TPU v7x, 32 devices: a whole 2x2x4 slice. The times are simulated.
32 devices in a mesh: dp: 8 (over z, core), shard: 4 (over y, x).
Axes of the slice: x: 2, y: 2, z: 4, core: 2. Of those that a mesh axis runs over, the one named last changes fastest.
Arguments:
- grads: bfloat16 [8, 256, 7168], P('dp', 'shard'), may hold values from -6 to 6
- errors: float32 [8, 256, 7168], P('dp', 'shard'), may hold values from -4 to 4
- q_prev: float32 [7168, 32], P('shard'), may hold values from -6 to 6
Outputs:
- new_errors: float32 [8, 256, 7168], P('dp', 'shard')
- q_new: float32 [7168, 32], P('shard')
All inputs are finite; a program needn't handle non-finite values.
Results may differ from a plain program's by a relative error of at most 0.0003.
Values sent between devices are 32-bit elements; how exact they have to be, the bound alone decides.
A program may use at most 64 MiB of HBM per device.

v0:
```python
import jax
import jax.numpy as jnp
from jax import lax
from jax.sharding import PartitionSpec as P


def per_device(grads, errors, q_prev):
    high = lax.Precision.HIGHEST
    merged = grads.astype(jnp.float32) + errors
    matrix = merged[0]
    width = matrix.shape[1]
    replicas = lax.axis_size("dp")
    partial_left = jnp.dot(
        matrix, lax.all_gather(q_prev, "shard", axis=0, tiled=True), precision=high
    )
    left = lax.psum(partial_left, "dp") / replicas
    local_gram = jnp.dot(left.T, left, precision=high)
    gram = lax.psum(local_gram, "shard")
    lower = jnp.linalg.cholesky(gram)
    p_hat = jax.scipy.linalg.solve_triangular(lower, left.T, lower=True).T
    own_term = jnp.dot(matrix.T, p_hat, precision=high)
    right_full = lax.psum(own_term, ("dp", "shard")) / replicas
    share = width // lax.axis_size("shard")
    q_mine = lax.dynamic_slice_in_dim(right_full, lax.axis_index("shard") * share, share, 0)
    approx = jnp.dot(p_hat, right_full.T, precision=high)
    return (merged - approx[None], q_mine)


def solution(mesh):
    in_specs = (P("dp", "shard", None), P("dp", "shard", None), P("shard", None))
    out_specs = (P("dp", "shard", None), P("shard", None))
    return jax.shard_map(
        per_device, mesh=mesh, in_specs=in_specs, out_specs=out_specs, check_vma=False
    )
```

profile of v0, /device:TPU:0, one launch (start us, length us, event | category | flops | bytes accessed | tf_op | source)
XLA Modules:
  0.0 215.5 jit_solution(16447065890858671314)
XLA Ops:
  7.2 0.0 all-reduce.2.cloned.1.call-start
  7.2 14.9 %all_gather.3 = f32[7168,32]{0,1:T(8,128)S(1)} all-gather(f32[1792,32]{0,1:T(8,128)} %param.5), channel_id=1, replica_groups=mesh['dp'=8,'shard'=4] {'shard'}, dimensions={0}, use_global_device_ids=true | all-gather | bytes 1146880 | tf_op jit(solution)/shard_map/all_gather | solution.py:14
  22.1 0.0 copy-start
  22.1 0.0 copy-start.1
  22.1 3.5 %fusion.3 = f32[64,32]{0,1:T(8,128)S(1)} fusion(f32[7168,32]{0,1:T(8,128)S(1)} %all_gather.3, f32[1,64,7168]{2,1,0:T(8,128)} %param.4, bf16[1,64,7168]{2,1,0:T(8,128)(2,1)} %param.3), kind=kOutput, calls=%fused_computation.4 | convolution fusion | flops 177078272 | bytes 3678208 | tf_op jit(solution)/shard_map/dot_general | solution.py:13
  25.6 27.6 %psum.21 = f32[64,32]{0,1:T(8,128)S(1)} all-reduce(f32[64,32]{0,1:T(8,128)S(1)} %fusion.3), channel_id=1, replica_groups=mesh['dp'=8,'shard'=4] {'dp'}, use_global_device_ids=true, to_apply=%region_0.0 | all-reduce | flops 2048 | bytes 16384 | tf_op jit(solution)/shard_map/psum | solution.py:16
  53.3 0.1 fusion.10
  53.4 15.1 %psum.22 = f32[32,32]{0,1:T(8,128)S(1)} all-reduce(f32[32,32]{0,1:T(8,128)S(1)} %fusion.10), channel_id=1, replica_groups=mesh['dp'=8,'shard'=4] {'shard'}, use_global_device_ids=true, to_apply=%region_1.0 | all-reduce | flops 1024 | bytes 8192 | tf_op jit(solution)/shard_map/psum | solution.py:18
  68.5 0.1 copy.6
  68.5 2.9 %cholesky.16 = f32[32,32]{1,0:T(8,128)S(1)} custom-call(f32[32,32]{1,0:T(8,128)S(1)} %fusion.8), custom_call_target="Cholesky" | custom-call | tf_op jit(solution)/shard_map/jit(cholesky)/cholesky | solution.py:19
  71.5 0.6 compare_reduce_fusion
  72.1 0.7 fusion.5
  72.8 2.5 %custom-call.7 = f32[1,32,32]{1,2,0:T(8,128)S(1)} custom-call(f32[1,32,32]{2,1,0:T(8,128)S(1)} %fusion.5), custom_call_target="InvertDiagBlocksLowerTriangular" | custom-call | tf_op jit(solution)/shard_map/jit(_solve_triangular)/triangular_solve | solution.py:20
  75.3 0.2 fusion.6
  75.5 0.0 copy-done
  75.5 0.0 copy-done.1
  75.5 2.2 %fusion.1 = f32[7168,32]{0,1:T(8,128)} fusion(f32[32,64]{1,0:T(8,128)S(1)} %fusion.6, f32[1,64,7168]{2,1,0:T(8,128)S(1)} %copy-done, bf16[1,64,7168]{2,1,0:T(8,128)(2,1)S(1)} %copy-done.1), kind=kOutput, calls=%fused_computation.2 | convolution fusion | flops 177078272 | bytes 3678208 | tf_op jit(solution)/shard_map/dot_general | solution.py:21
  77.7 0.0 all-reduce.2.cloned.1.call-update
  77.7 126.0 %all-reduce.2.cloned.1.call-done = f32[7168,32]{0,1:T(8,128)} async-done(((f32[7168,32]{0,1:T(8,128)}), f32[7168,32]{0,1:T(8,128)}) %all-reduce.2.cloned.1.call-update) | async-done | bytes 917520 | tf_op jit(solution)/shard_map/psum | solution.py:22
  203.7 0.0 copy-start.2
  203.7 1.3 broadcast_multiply_fusion
  205.0 0.7 constant_dynamic-slice_fusion
  205.7 0.0 copy-done.2
  205.7 2.9 %fusion = f32[1,64,7168]{2,1,0:T(8,128)} fusion(f32[32,64]{1,0:T(8,128)S(1)} %fusion.6, f32[1,64,7168]{2,1,0:T(8,128)S(1)} %copy-done, bf16[1,64,7168]{2,1,0:T(8,128)(2,1)S(1)} %copy-done.1, f32[7168,32]{0,1:T(8,128)S(1)} %copy-done.2), kind=kOutput, calls=%fused_computation.1 | convolution fusion | flops 177766400 | bytes 5513216 | tf_op jit(solution)/shard_map/dot_general | solution.py:25
  (2 shorter events, 0.0 us)
Async XLA Ops:
  7.2 196.5 %all-reduce.2.cloned.1.call-start = ((), (), s32[]{:S(2)}) async-start(), calls=%async_computation | async-start | bytes 1835008 | tf_op jit(solution)/shard_map/psum | solution.py:22
  22.1 53.4 %copy-start = (f32[1,64,7168]{2,1,0:T(8,128)S(1)}, f32[1,64,7168]{2,1,0:T(8,128)}, u32[]{:S(2)}) copy-start(f32[1,64,7168]{2,1,0:T(8,128)} %param.4) | copy-start | bytes 5505028
  22.1 53.4 %copy-start.1 = (bf16[1,64,7168]{2,1,0:T(8,128)(2,1)S(1)}, bf16[1,64,7168]{2,1,0:T(8,128)(2,1)}, u32[]{:S(2)}) copy-start(bf16[1,64,7168]{2,1,0:T(8,128)(2,1)} %param.3) | copy-start | bytes 2752516
  203.7 2.0 copy-start.2
Sparse Core Ops, SparseCore 0:
  77.8 125.8 all-reduce.1
where the time goes:
time: 216 us
  waiting for transfers between devices  126 us (58%)
  blocking collectives  57.6 us (27%)
  between operations  14.1 us (7%)
  matrix products  9 us (4%)
  other arithmetic  8.04 us (4%)
    psum x1, waiting for transfers between devices, per_device(): right_full = lax.psum(own_term, ('dp', 'shard')) / replicas  126 us
    psum x1, blocking collectives, per_device(): left = lax.psum(partial_left, 'dp') / replicas  27.6 us
    psum x1, blocking collectives, per_device(): gram = lax.psum(local_gram, 'shard')  15.1 us
    all_gather x1, blocking collectives, per_device(): lax.all_gather(q_prev, 'shard', axis=0, tiled=True)  14.9 us
  transfers between devices with their start and end apart: 1, of which 1 were waited for; matrix products, arithmetic and copies ran while one was open for 0% of the time, Pallas kernels for 0%

commit v1 on v0

v1 whole, which is shorter than its diff:
```python
import functools

import jax
import jax.numpy as jnp
from jax import lax
from jax.experimental import pallas as pl
from jax.experimental.pallas import tpu as pltpu
from jax.sharding import PartitionSpec as P

MESH = pl.DeviceIdType.MESH
HIGH = lax.Precision.HIGHEST
F32 = jnp.float32
BF16 = jnp.bfloat16
NT = (((1,), (1,)), ((), ()))
NN = (((1,), (0,)), ((), ()))


def dot(a, b, dims=NN, precision=None):
    return lax.dot_general(a, b, dims, precision=precision, preferred_element_type=F32)


def halves(x):
    hi = x.astype(BF16)
    return hi, (x - hi.astype(F32)).astype(BF16)


def inverse_factor(gram):
    n = gram.shape[0]
    rows = lax.broadcasted_iota(jnp.int32, (n, 128), 0)
    lanes = lax.broadcasted_iota(jnp.int32, (n, 128), 1)
    work = jnp.where(lanes == rows + n, 1.0, gram)
    for j in range(n):
        pivot = work[j : j + 1, :]
        column = work[:, j : j + 1]
        scale = column / pivot[:, j : j + 1]
        work = jnp.where(rows > j, work - scale * pivot, work)
    diag = jnp.sum(jnp.where(lanes == rows, work, 0.0), axis=1, keepdims=True)
    work = work * lax.rsqrt(diag)
    return work[:, n : 2 * n]


def kernel(
    dims, g_hbm, e_hbm, q_ref, out_hbm, qnew_ref,
    g_v, e_v, m2, mf, q_all, pbuf, gbuf, w_a, w_b, w_c, w_r, r_buf, z_r, z_full, y_all, out_v,
    in_sem, q_s, q_r, qf_s, qf_r, p_s, p_r, g_s, g_r, c_s, c_r, w_s, w_rs, zr_s, zr_r, za_s, za_r,
    y_s, y_r, yc_s, yc_r, out_sem,
):
    n_dp, n_sh, nz, zrows, split_z, aligned, width = dims
    rank = q_ref.shape[0]
    pieces = 2 * n_sh
    d = lax.axis_index("dp")
    s = lax.axis_index("shard")
    z = d // 2
    c = d % 2
    oc = 1 - c
    sib = d + 1 - 2 * c

    load_g = pltpu.make_async_copy(g_hbm.at[0], g_v, in_sem.at[0])
    load_e = pltpu.make_async_copy(e_hbm.at[0], e_v, in_sem.at[1])
    load_g.start()
    load_e.start()

    def at_dp(i):
        return lax.rem(d + i, n_dp)

    def at_sh(i):
        return lax.rem(s + i, n_sh)

    def at_z(i):
        return lax.rem(z + i, nz)

    barrier = pltpu.get_barrier_semaphore()
    for i in range(1, n_dp):
        pl.semaphore_signal(barrier, inc=1, device_id=(at_dp(i), s), device_id_type=MESH)
    for i in range(1, n_sh):
        pl.semaphore_signal(barrier, inc=1, device_id=(d, at_sh(i)), device_id_type=MESH)
    for h in range(2):
        q_all[2 * s + h] = q_ref[:, h * width : (h + 1) * width]
    pl.semaphore_wait(barrier, n_dp - 1 + n_sh - 1)

    def remote(src, dst, send, recv, target):
        return pltpu.make_async_remote_copy(
            src_ref=src, dst_ref=dst, send_sem=send, recv_sem=recv, device_id=target, device_id_type=MESH
        )

    sends = []

    def send(src, dst, send_sem, recv_sem, target):
        copy = remote(src, dst, send_sem, recv_sem, target)
        copy.start()
        sends.append(copy)

    def arrived(dst, send_sem, recv_sem):
        remote(dst, dst, send_sem, recv_sem, (sib, s)).wait_recv()

    mine = 2 * s + c
    for i in range(1, n_sh):
        send(q_all.at[mine], q_all.at[mine], q_s.at[i], q_r.at[s], (d, at_sh(i)))

    load_g.wait()
    load_e.wait()
    for k in range(pieces):
        span = slice(k * width, (k + 1) * width)
        m = g_v[:, span].astype(F32) + e_v[:, span]
        hi, lo = halves(m)
        mf[k] = m
        m2[k, : m.shape[0]] = hi
        m2[k, m.shape[0] :] = lo

    def left_term(k):
        hi, lo = halves(q_all[k])
        return dot(jnp.concatenate([hi, lo], axis=0), m2[k], NT)

    acc = left_term(2 * s) + left_term(2 * s + 1)
    for i in range(1, n_sh):
        o = at_sh(i)
        k = 2 * o + c
        arrived(q_all.at[k], q_s.at[i], q_r.at[o])
        send(q_all.at[k], q_all.at[k], qf_s.at[i], qf_r.at[o], (sib, s))
        acc = acc + left_term(k)
    for i in range(1, n_sh):
        o = at_sh(i)
        k = 2 * o + oc
        arrived(q_all.at[k], qf_s.at[i], qf_r.at[o])
        acc = acc + left_term(k)
    acc = acc[:rank] + acc[rank:]
    n_rows = mf.shape[1]
    part = acc[:, :n_rows] + acc[:, n_rows:]
    half = rank // 2

    pbuf[d] = jnp.concatenate([part[:half], part[half:]], axis=1)
    for i in range(1, n_dp):
        send(pbuf.at[d], pbuf.at[d], p_s.at[i], p_r.at[d], (at_dp(i), s))
    for i in range(1, n_dp):
        o = at_dp(i)
        arrived(pbuf.at[o], p_s.at[i], p_r.at[o])
    total = pbuf[0]
    for k in range(1, n_dp):
        total = total + pbuf[k]
    total = total * (1.0 / n_dp)
    pt = jnp.concatenate([total[:, :n_rows], total[:, n_rows:]], axis=0)

    padded = jnp.concatenate([pt, jnp.zeros((128 - rank, n_rows), F32)], axis=0)
    gbuf[s] = dot(pt, padded, NT, HIGH)
    for i in range(1, n_sh):
        send(gbuf.at[s], gbuf.at[s], g_s.at[i], g_r.at[s], (d, at_sh(i)))

    twice = jnp.concatenate([pt, pt], axis=1) * (1.0 / n_dp)
    p_hi, p_lo = halves(twice)
    p2 = jnp.concatenate([p_hi, p_lo], axis=0)

    def w_term(k):
        t = dot(p2, m2[k])
        return t[:rank] + t[rank:]

    order = list(range(1, n_sh)) + [0]
    for i in order:
        o = at_sh(i)
        w_a[o] = w_term(2 * o + oc)
        send(w_a.at[o], w_b.at[o], c_s.at[i], c_r.at[o], (sib, s))
    for i in order:
        o = at_sh(i)
        own = w_term(2 * o + c)
        arrived(w_b.at[o], c_s.at[i], c_r.at[o])
        if i == 0:
            w_r[s] = own + w_b[s]
        else:
            w_c[o] = own + w_b[o]
            send(w_c.at[o], w_r.at[s], w_s.at[i], w_rs.at[s], (d, at_sh(i)))

    for i in range(1, n_sh):
        o = at_sh(i)
        arrived(gbuf.at[o], g_s.at[i], g_r.at[o])
    gram = gbuf[0]
    for k in range(1, n_sh):
        gram = gram + gbuf[k]
    linv = inverse_factor(gram)
    p_hat_t = dot(linv, pt, NN, HIGH)
    three = jnp.concatenate([p_hat_t, p_hat_t, p_hat_t], axis=0)
    rounded = three.astype(BF16).astype(F32)
    row = lax.broadcasted_iota(jnp.int32, three.shape, 0)
    ph3 = jnp.where(row < 2 * rank, rounded, three - rounded).T.astype(BF16)

    for i in range(1, n_sh):
        o = at_sh(i)
        arrived(w_r.at[o], w_s.at[i], w_rs.at[o])
    r = w_r[0]
    for k in range(1, n_sh):
        r = r + w_r[k]

    if split_z:
        for k in range(nz):
            r_buf[k] = r[k * zrows : (k + 1) * zrows]
        z_r[z] = r_buf[z]
        for i in range(1, nz):
            o = at_z(i)
            send(r_buf.at[o], z_r.at[z], zr_s.at[i], zr_r.at[z], (2 * o + c, s))
    else:
        z_r[z] = r
        for i in range(1, nz):
            o = at_z(i)
            send(z_r.at[z], z_r.at[z], zr_s.at[i], zr_r.at[z], (2 * o + c, s))
    for i in range(1, nz):
        o = at_z(i)
        arrived(z_r.at[o], zr_s.at[i], zr_r.at[o])
    r = z_r[0]
    for k in range(1, nz):
        r = r + z_r[k]
    if split_z:
        z_full[z] = r
        for i in range(1, nz):
            o = at_z(i)
            send(z_full.at[z], z_full.at[z], za_s.at[i], za_r.at[z], (2 * o + c, s))
        for i in range(1, nz):
            o = at_z(i)
            arrived(z_full.at[o], za_s.at[i], za_r.at[o])
        r = jnp.concatenate([z_full[k] for k in range(nz)], axis=0)

    y_all[mine] = dot(linv, r, NN, HIGH)
    send(y_all.at[mine], y_all.at[mine], yc_s.at[0], yc_r.at[s], (sib, s))
    for i in range(1, n_sh):
        send(y_all.at[mine], y_all.at[mine], y_s.at[i], y_r.at[s], (d, at_sh(i)))

    stores = []

    def finish(k, slot):
        hi, lo = halves(y_all[k])
        mf[k] = mf[k] - dot(ph3, jnp.concatenate([hi, lo, hi], axis=0))
        if aligned:
            start = pl.multiple_of(k * width, 128)
            copy = pltpu.make_async_copy(mf.at[k], out_hbm.at[0, :, pl.ds(start, width)], out_sem.at[slot])
            copy.start()
            stores.append(copy)

    finish(mine, 0)
    arrived(y_all.at[2 * s + oc], yc_s.at[0], yc_r.at[s])
    finish(2 * s + oc, 1)
    for h in range(2):
        qnew_ref[:, h * width : (h + 1) * width] = y_all[2 * s + h]
    for i in range(1, n_sh):
        o = at_sh(i)
        k = 2 * o + c
        arrived(y_all.at[k], y_s.at[i], y_r.at[o])
        send(y_all.at[k], y_all.at[k], yc_s.at[i], yc_r.at[o], (sib, s))
        finish(k, 2 * i)
    for i in range(1, n_sh):
        o = at_sh(i)
        k = 2 * o + oc
        arrived(y_all.at[k], yc_s.at[i], yc_r.at[o])
        finish(k, 2 * i + 1)
    if not aligned:
        for k in range(pieces):
            out_v[:, k * width : (k + 1) * width] = mf[k]
        copy = pltpu.make_async_copy(out_v, out_hbm.at[0], out_sem.at[0])
        copy.start()
        stores.append(copy)
    for copy in sends:
        copy.wait_send()
    for copy in stores:
        copy.wait()


def per_device(n_dp, n_sh, grads, errors, q_prev):
    _, n_rows, full = grads.shape
    share, rank = q_prev.shape
    width = share // 2
    nz = n_dp // 2
    split_z = rank % (8 * nz) == 0
    zrows = rank // nz if split_z else rank
    aligned = width % 128 == 0
    pieces = 2 * n_sh
    dims = (n_dp, n_sh, nz, zrows, split_z, aligned, width)
    vm = pltpu.VMEM
    dma = pltpu.SemaphoreType.DMA
    small = (8, 128)
    scratch = [
        vm((n_rows, full), BF16),
        vm((n_rows, full), F32),
        vm((pieces, 2 * n_rows, width), BF16),
        vm((pieces, n_rows, width), F32),
        vm((pieces, rank, width), F32),
        vm((n_dp, rank // 2, 2 * n_rows), F32),
        vm((n_sh, rank, 128), F32),
        vm((n_sh, rank, width), F32),
        vm((n_sh, rank, width), F32),
        vm((n_sh, rank, width), F32),
        vm((n_sh, rank, width), F32),
        vm((nz, zrows, width) if split_z else small, F32),
        vm((nz, zrows, width), F32),
        vm((nz, zrows, width) if split_z else small, F32),
        vm((pieces, rank, width), F32),
        vm(small if aligned else (n_rows, full), F32),
        dma((2,)),
    ]
    for count in (n_sh, n_sh, n_dp, n_sh, n_sh, n_sh, nz, nz, n_sh, n_sh):
        scratch += [dma((count,)), dma((count,))]
    scratch.append(dma((pieces,)))
    out, q_new = pl.pallas_call(
        functools.partial(kernel, dims),
        out_shape=(
            jax.ShapeDtypeStruct((1, n_rows, full), F32),
            jax.ShapeDtypeStruct((rank, share), F32),
        ),
        in_specs=[
            pl.BlockSpec(memory_space=pl.ANY),
            pl.BlockSpec(memory_space=pl.ANY),
            pl.BlockSpec(memory_space=pltpu.VMEM),
        ],
        out_specs=(pl.BlockSpec(memory_space=pl.ANY), pl.BlockSpec(memory_space=pltpu.VMEM)),
        scratch_shapes=scratch,
        compiler_params=pltpu.CompilerParams(
            collective_id=0, has_side_effects=True, vmem_limit_bytes=48 * 1024 * 1024
        ),
        cost_estimate=pl.CostEstimate(
            flops=18 * n_rows * full * rank, bytes_accessed=10 * n_rows * full, transcendentals=0
        ),
    )(grads, errors, q_prev.T)
    return out, q_new.T


def solution(mesh):
    in_specs = (P("dp", "shard", None), P("dp", "shard", None), P("shard", None))
    out_specs = (P("dp", "shard", None), P("shard", None))
    return jax.shard_map(
        functools.partial(per_device, mesh.shape["dp"], mesh.shape["shard"]),
        mesh=mesh, in_specs=in_specs, out_specs=out_specs, check_vma=False,
    )
```

time: 216 us -> 49.8 us (0.23)
  waiting for transfers between devices: 126 us -> 0 us
  blocking collectives: 57.6 us -> 0 us
  Pallas kernels: 0 us -> 43.3 us
  between operations: 14.1 us -> 0.65 us
  matrix products: 9 us -> 0 us
  other arithmetic: 8.04 us -> 0 us
  local copies, waits for them, and re-layouts: 0.8 us -> 5.53 us
    psum x1 -> x0, waiting for transfers between devices: 126 us -> none  [per_device(): right_full = lax.psum(own_term, ('dp', 'shard')) / replicas]
    pallas_call x0 -> x1, Pallas kernels: none -> 43.3 us  [per_device(): pl.pallas_call(functools.partial(kernel, dims), out_shape=(jax.ShapeDtype...]
    psum x2 -> x0, blocking collectives: 42.7 us -> none  [the longest x1 27.6 us: per_device(): left = lax.psum(partial_left, 'dp') / replicas]
    all_gather x1 -> x0, blocking collectives: 14.9 us -> none  [per_device(): lax.all_gather(q_prev, 'shard', axis=0, tiled=True)]
    dot_general x4 -> x0, matrix products: 8.79 us -> none  [the longest x1 3.52 us: per_device(): jnp.dot(matrix, lax.all_gather(q_prev, 'shard', axis=0, tiled=True), prec...]
    another operation x5 -> x0, other arithmetic: 6.71 us -> none  [the longest x3 3.59 us: per_device(): lower = jnp.linalg.cholesky(gram)]
    unnamed x6 -> x8, local copies, waits for them, and re-layouts: 0.01 us -> 5.53 us
  transfers between devices with their start and end apart: 1 -> 0, of which waited for: 1 -> 0; matrix products, arithmetic and copies ran while one was open for 0% -> 0% of each run, Pallas kernels for 0% -> 0%
where the time goes in v1:
time: 49.8 us; the launch traced here: 49.5 us
  Pallas kernels  43.3 us (87%)
  local copies, waits for them, and re-layouts  5.53 us (11%)
  between operations  0.65 us (1%)
    pallas_call x1, Pallas kernels, per_device(): pl.pallas_call(functools.partial(kernel, dims), out_shape=(jax.ShapeDtype...  43.3 us
    unnamed x8, local copies, waits for them, and re-layouts  5.53 us

profile of v1, /device:TPU:0, one launch (start us, length us, event | category | flops | bytes accessed | tf_op | source)
XLA Modules:
  0.0 49.5 jit_solution(14150134921682305169)
XLA Ops:
  0.6 0.0 copy-start
  0.6 1.5 %copy-done = f32[1,64,7168]{2,1,0:T(8,128)S(1)} copy-done((f32[1,64,7168]{2,1,0:T(8,128)S(1)}, f32[1,64,7168]{2,1,0:T(8,128)}, u32[]{:S(2)}) %copy-start) | copy-done | bytes 1835032
  2.1 0.0 copy-start.1
  2.1 1.2 %copy-done.1 = bf16[1,64,7168]{2,1,0:T(8,128)(2,1)S(1)} copy-done((bf16[1,64,7168]{2,1,0:T(8,128)(2,1)S(1)}, bf16[1,64,7168]{2,1,0:T(8,128)(2,1)}, u32[]{:S(2)}) %copy-start.1) | copy-done | bytes 917528
  3.3 0.0 copy-start.2
  3.3 0.9 %copy-done.2 = f32[1792,32]{0,1:T(8,128)S(1)} copy-done((f32[1792,32]{0,1:T(8,128)S(1)}, f32[1792,32]{0,1:T(8,128)}, u32[]{:S(2)}) %copy-start.2) | copy-done | bytes 229400
  4.2 43.3 %shard_map.50 = (f32[1,64,7168]{2,1,0:T(8,128)S(1)}, f32[32,1792]{1,0:T(8,128)S(1)}) custom-call(bf16[1,64,7168]{2,1,0:T(8,128)(2,1)S(1)} %copy-done.1, f32[1,64,7168]{2,1,0:T(8,128)S(1)} %copy-done, f32[32,1792]{1,0:T(8,128)S(1)} %bitcast.2), custom_call_target="tpu_custom_call" | custom-call | flops 264241152 | bytes 4587520 | tf_op jit(solution)/shard_map/pallas_call | solution.py:298
  47.5 1.2 %copy.7 = f32[1,64,7168]{2,1,0:T(8,128)} copy(f32[1,64,7168]{2,1,0:T(8,128)S(1)} %get-tuple-element.8) | data formatting | bytes 3670016
  48.8 0.7 %copy.8 = f32[1792,32]{0,1:T(8,128)} copy(f32[1792,32]{0,1:T(8,128)S(1)} %bitcast.3) | data formatting | bytes 458752
Async XLA Ops:
  0.6 1.5 %copy-start = (f32[1,64,7168]{2,1,0:T(8,128)S(1)}, f32[1,64,7168]{2,1,0:T(8,128)}, u32[]{:S(2)}) copy-start(f32[1,64,7168]{2,1,0:T(8,128)} %e_hbm.1) | copy-start | bytes 5505028
  2.1 1.2 %copy-start.1 = (bf16[1,64,7168]{2,1,0:T(8,128)(2,1)S(1)}, bf16[1,64,7168]{2,1,0:T(8,128)(2,1)}, u32[]{:S(2)}) copy-start(bf16[1,64,7168]{2,1,0:T(8,128)(2,1)} %g_hbm.1) | copy-start | bytes 2752516
  3.3 0.9 %copy-start.2 = (f32[1792,32]{0,1:T(8,128)S(1)}, f32[1792,32]{0,1:T(8,128)}, u32[]{:S(2)}) copy-start(f32[1792,32]{0,1:T(8,128)} %param.5) | copy-start | bytes 688132

commit v2 on v1

--- a/solution.py
+++ b/solution.py
@@ -29,24 +29,28 @@
     rows = lax.broadcasted_iota(jnp.int32, (n, 128), 0)
     lanes = lax.broadcasted_iota(jnp.int32, (n, 128), 1)
     work = jnp.where(lanes == rows + n, 1.0, gram)
-    for j in range(n):
-        pivot = work[j : j + 1, :]
-        column = work[:, j : j + 1]
-        scale = column / pivot[:, j : j + 1]
-        work = jnp.where(rows > j, work - scale * pivot, work)
+    block = 8
+    for first in range(0, n, block):
+        columns = [jnp.broadcast_to(work[:, first + t : first + t + 1], (n, 128)) for t in range(block)]
+        for t in range(block):
+            j = first + t
+            scale = jnp.where(rows > j, columns[t] * (1.0 / columns[t][j : j + 1]), 0.0)
+            for u in range(t + 1, block):
+                columns[u] = columns[u] - scale * columns[u][j : j + 1]
+            work = work - scale * work[j : j + 1]
     diag = jnp.sum(jnp.where(lanes == rows, work, 0.0), axis=1, keepdims=True)
     work = work * lax.rsqrt(diag)
     return work[:, n : 2 * n]
 
 
 def kernel(
-    dims, g_hbm, e_hbm, q_ref, out_hbm, qnew_ref,
-    g_v, e_v, m2, mf, q_all, pbuf, gbuf, w_a, w_b, w_c, w_r, r_buf, z_r, z_full, y_all, out_v,
+    dims, g_hbm, e_hbm, q_hbm, out_hbm, qnew_ref,
+    g_v, e_v, q_v, m2, mf, q_all, pbuf, gbuf, w_a, w_b, w_c, w_r, r_buf, z_r, z_full, y_all, out_v,
     in_sem, q_s, q_r, qf_s, qf_r, p_s, p_r, g_s, g_r, c_s, c_r, w_s, w_rs, zr_s, zr_r, za_s, za_r,
     y_s, y_r, yc_s, yc_r, out_sem,
 ):
     n_dp, n_sh, nz, zrows, split_z, aligned, width = dims
-    rank = q_ref.shape[0]
+    rank = q_hbm.shape[0]
     pieces = 2 * n_sh
     d = lax.axis_index("dp")
     s = lax.axis_index("shard")
@@ -57,6 +61,18 @@
 
     load_g = pltpu.make_async_copy(g_hbm.at[0], g_v, in_sem.at[0])
     load_e = pltpu.make_async_copy(e_hbm.at[0], e_v, in_sem.at[1])
+    q_loads = []
+    if aligned:
+        for h in range(2):
+            half_copy = pltpu.make_async_copy(
+                q_hbm.at[:, h * width : (h + 1) * width], q_all.at[2 * s + h], in_sem.at[2 + h]
+            )
+            half_copy.start()
+            q_loads.append(half_copy)
+    else:
+        whole_copy = pltpu.make_async_copy(q_hbm, q_v, in_sem.at[2])
+        whole_copy.start()
+        q_loads.append(whole_copy)
     load_g.start()
     load_e.start()
 
@@ -74,8 +90,11 @@
         pl.semaphore_signal(barrier, inc=1, device_id=(at_dp(i), s), device_id_type=MESH)
     for i in range(1, n_sh):
         pl.semaphore_signal(barrier, inc=1, device_id=(d, at_sh(i)), device_id_type=MESH)
-    for h in range(2):
-        q_all[2 * s + h] = q_ref[:, h * width : (h + 1) * width]
+    for q_load in q_loads:
+        q_load.wait()
+    if not aligned:
+        for h in range(2):
+            q_all[2 * s + h] = q_v[:, h * width : (h + 1) * width]
     pl.semaphore_wait(barrier, n_dp - 1 + n_sh - 1)
 
     def remote(src, dst, send, recv, target):
@@ -276,6 +295,7 @@
     scratch = [
         vm((n_rows, full), BF16),
         vm((n_rows, full), F32),
+        vm(small if aligned else (rank, share), F32),
         vm((pieces, 2 * n_rows, width), BF16),
         vm((pieces, n_rows, width), F32),
         vm((pieces, rank, width), F32),
@@ -290,7 +310,7 @@
         vm((nz, zrows, width) if split_z else small, F32),
         vm((pieces, rank, width), F32),
         vm(small if aligned else (n_rows, full), F32),
-        dma((2,)),
+        dma((4,)),
     ]
     for count in (n_sh, n_sh, n_dp, n_sh, n_sh, n_sh, nz, nz, n_sh, n_sh):
         scratch += [dma((count,)), dma((count,))]
@@ -302,14 +322,14 @@
             jax.ShapeDtypeStruct((rank, share), F32),
         ),
         in_specs=[
-            pl.BlockSpec(memory_space=pl.ANY),
-            pl.BlockSpec(memory_space=pl.ANY),
-            pl.BlockSpec(memory_space=pltpu.VMEM),
+            pl.BlockSpec(memory_space=pltpu.HBM),
+            pl.BlockSpec(memory_space=pltpu.HBM),
+            pl.BlockSpec(memory_space=pltpu.HBM),
         ],
         out_specs=(pl.BlockSpec(memory_space=pl.ANY), pl.BlockSpec(memory_space=pltpu.VMEM)),
         scratch_shapes=scratch,
         compiler_params=pltpu.CompilerParams(
-            collective_id=0, has_side_effects=True, vmem_limit_bytes=48 * 1024 * 1024
+            collective_id=0, has_side_effects=True, vmem_limit_bytes=63 * 1024 * 1024
         ),
         cost_estimate=pl.CostEstimate(
             flops=18 * n_rows * full * rank, bytes_accessed=10 * n_rows * full, transcendentals=0

time: 49.8 us -> 48.8 us (0.980)
  local copies, waits for them, and re-layouts: 5.53 us -> 3.59 us
  Pallas kernels: 43.3 us -> 44 us
    unnamed x8 -> x4, local copies, waits for them, and re-layouts: 5.53 us -> 3.59 us
    pallas_call x1, Pallas kernels: 43.3 us -> 44 us  [per_device(): pl.pallas_call(functools.partial(kernel, dims), out_shape=(jax.ShapeDtype...]
where the time goes in v2:
time: 48.8 us; the launch traced here: 48.3 us
  Pallas kernels  44 us (90%)
  local copies, waits for them, and re-layouts  3.59 us (7%)
  between operations  0.65 us (1%)
    pallas_call x1, Pallas kernels, per_device(): pl.pallas_call(functools.partial(kernel, dims), out_shape=(jax.ShapeDtype...  44 us
    unnamed x4, local copies, waits for them, and re-layouts  3.59 us

profile of v2, /device:TPU:0, one launch (start us, length us, event | category | flops | bytes accessed | tf_op | source)
XLA Modules:
  0.0 48.3 jit_solution(7816479929767429752)
XLA Ops:
  0.6 44.0 %shard_map.50 = (f32[1,64,7168]{2,1,0:T(8,128)}, f32[32,1792]{1,0:T(8,128)}) custom-call(bf16[1,64,7168]{2,1,0:T(8,128)(2,1)} %g_hbm.1, f32[1,64,7168]{2,1,0:T(8,128)} %e_hbm.1, f32[32,1792]{1,0:T(8,128)} %bitcast.2), custom_call_target="tpu_custom_call" | custom-call | flops 264241152 | bytes 4587520 | tf_op jit(solution)/shard_map/pallas_call | solution.py:318
  44.7 0.0 copy-start
  44.7 2.9 %copy.7 = f32[1,64,7168]{2,1,0:T(8,128)} copy(f32[1,64,7168]{2,1,0:T(8,128)} %get-tuple-element.8) | data formatting | bytes 3670016
  47.6 0.0 copy-done
  47.6 0.7 %copy.8 = f32[1792,32]{0,1:T(8,128)} copy(f32[1792,32]{0,1:T(8,128)S(1)} %bitcast.3) | data formatting | bytes 458752
Async XLA Ops:
  44.7 2.9 %copy-start = (f32[32,1792]{1,0:T(8,128)S(1)}, f32[32,1792]{1,0:T(8,128)}, u32[]{:S(2)}) copy-start(f32[32,1792]{1,0:T(8,128)} %get-tuple-element.5) | copy-start | bytes 688132

commit v3 on v2

v3 whole, which is shorter than its diff:
```python
import functools

import jax
import jax.numpy as jnp
from jax import lax
from jax.experimental import pallas as pl
from jax.experimental.pallas import tpu as pltpu
from jax.sharding import PartitionSpec as P

MESH = pl.DeviceIdType.MESH
HIGH = lax.Precision.HIGHEST
F32 = jnp.float32
BF16 = jnp.bfloat16
NT = (((1,), (1,)), ((), ()))
NN = (((1,), (0,)), ((), ()))
N_CHUNKS = 2
PLACE_PARTS = 4


def dot(a, b, dims=NN, precision=None):
    return lax.dot_general(a, b, dims, precision=precision, preferred_element_type=F32)


def halves(x):
    hi = x.astype(BF16)
    return hi, (x - hi.astype(F32)).astype(BF16)


def inverse_factor(gram):
    n = gram.shape[0]
    rows = lax.broadcasted_iota(jnp.int32, (n, 128), 0)
    lanes = lax.broadcasted_iota(jnp.int32, (n, 128), 1)
    work = jnp.where(lanes == rows + n, 1.0, gram)
    block = 8
    for first in range(0, n, block):
        columns = [jnp.broadcast_to(work[:, first + t : first + t + 1], (n, 128)) for t in range(block)]
        for t in range(block):
            j = first + t
            scale = jnp.where(rows > j, columns[t] * (1.0 / columns[t][j : j + 1]), 0.0)
            for u in range(t + 1, block):
                columns[u] = columns[u] - scale * columns[u][j : j + 1]
            work = work - scale * work[j : j + 1]
    diag = jnp.sum(jnp.where(lanes == rows, work, 0.0), axis=1, keepdims=True)
    work = work * lax.rsqrt(diag)
    return work[:, n : 2 * n]


def kernel(
    dims, chunks, g_hbm, e_hbm, q_hbm, out_hbm, qnew_hbm,
    g_v, e_v, q_v, m2, mf, q_all, pbuf, gbuf, w_a, w_b, w_c, w_r, r_buf, z_r, z_full, y_all, out_v, qn_v,
    in_sem, q_s, q_r, qf_s, qf_r, p_s, p_r, g_s, g_r, c_s, c_r, w_s, w_rs, zr_s, zr_r, za_s, za_r,
    y_s, y_r, yc_s, yc_r, out_sem, qn_sem,
):
    n_dp, n_sh, nz, zrows, split_z, aligned, width = dims
    spans = [pl.ds(lo, hi - lo) for lo, hi in chunks]
    n_ch = len(chunks)
    rank = q_hbm.shape[0]
    pieces = 2 * n_sh
    d = lax.axis_index("dp")
    s = lax.axis_index("shard")
    z = d // 2
    c = d % 2
    oc = 1 - c
    sib = d + 1 - 2 * c

    load_g = pltpu.make_async_copy(g_hbm.at[0], g_v, in_sem.at[0])
    load_e = pltpu.make_async_copy(e_hbm.at[0], e_v, in_sem.at[1])
    q_loads = []
    if aligned:
        for h in range(2):
            half_copy = pltpu.make_async_copy(
                q_hbm.at[:, h * width : (h + 1) * width], q_all.at[2 * s + h], in_sem.at[2 + h]
            )
            half_copy.start()
            q_loads.append(half_copy)
    else:
        whole_copy = pltpu.make_async_copy(q_hbm, q_v, in_sem.at[2])
        whole_copy.start()
        q_loads.append(whole_copy)
    load_g.start()
    load_e.start()

    def at_dp(i):
        return lax.rem(d + i, n_dp)

    def at_sh(i):
        return lax.rem(s + i, n_sh)

    def at_z(i):
        return lax.rem(z + i, nz)

    barrier = pltpu.get_barrier_semaphore()
    for i in range(1, n_dp):
        pl.semaphore_signal(barrier, inc=1, device_id=(at_dp(i), s), device_id_type=MESH)
    for i in range(1, n_sh):
        pl.semaphore_signal(barrier, inc=1, device_id=(d, at_sh(i)), device_id_type=MESH)
    for q_load in q_loads:
        q_load.wait()
    if not aligned:
        for h in range(2):
            q_all[2 * s + h] = q_v[:, h * width : (h + 1) * width]
    pl.semaphore_wait(barrier, n_dp - 1 + n_sh - 1)

    def remote(src, dst, send, recv, target):
        return pltpu.make_async_remote_copy(
            src_ref=src, dst_ref=dst, send_sem=send, recv_sem=recv, device_id=target, device_id_type=MESH
        )

    sends = []

    def send(src, dst, send_sem, recv_sem, target):
        copy = remote(src, dst, send_sem, recv_sem, target)
        copy.start()
        sends.append(copy)

    def arrived(dst, send_sem, recv_sem):
        remote(dst, dst, send_sem, recv_sem, (sib, s)).wait_recv()

    mine = 2 * s + c
    other = 2 * s + oc
    for ch, span in enumerate(spans):
        part = q_all.at[mine, :, span]
        for i in range(1, n_sh):
            send(part, part, q_s.at[ch, i], q_r.at[ch, s], (d, at_sh(i)))

    load_g.wait()
    load_e.wait()
    for k in range(pieces):
        cols = slice(k * width, (k + 1) * width)
        m = g_v[:, cols].astype(F32) + e_v[:, cols]
        hi, lo = halves(m)
        mf[k] = m
        m2[k, : m.shape[0]] = hi
        m2[k, m.shape[0] :] = lo

    def left_term(k, span):
        hi, lo = halves(q_all[k, :, span])
        return dot(jnp.concatenate([hi, lo], axis=0), m2[k, :, span], NT)

    acc = left_term(2 * s, pl.ds(0, width)) + left_term(2 * s + 1, pl.ds(0, width))
    for ch, span in enumerate(spans):
        for i in range(1, n_sh):
            o = at_sh(i)
            part = q_all.at[2 * o + c, :, span]
            arrived(part, q_s.at[ch, i], q_r.at[ch, o])
            send(part, part, qf_s.at[ch, i], qf_r.at[ch, o], (sib, s))
        for i in range(1, n_sh):
            acc = acc + left_term(2 * at_sh(i) + c, span)
        for i in range(1, n_sh):
            o = at_sh(i)
            arrived(q_all.at[2 * o + oc, :, span], qf_s.at[ch, i], qf_r.at[ch, o])
            acc = acc + left_term(2 * o + oc, span)
    acc = acc[:rank] + acc[rank:]
    n_rows = mf.shape[1]
    part = acc[:, :n_rows] + acc[:, n_rows:]
    half = rank // 2

    pbuf[d] = jnp.concatenate([part[:half], part[half:]], axis=1)
    for i in range(1, n_dp):
        send(pbuf.at[d], pbuf.at[d], p_s.at[i], p_r.at[d], (at_dp(i), s))
    for i in range(1, n_dp):
        o = at_dp(i)
        arrived(pbuf.at[o], p_s.at[i], p_r.at[o])
    total = pbuf[0]
    for k in range(1, n_dp):
        total = total + pbuf[k]
    total = total * (1.0 / n_dp)
    pt = jnp.concatenate([total[:, :n_rows], total[:, n_rows:]], axis=0)

    twice = jnp.concatenate([pt, pt], axis=1) * (1.0 / n_dp)
    p_hi, p_lo = halves(twice)
    p2 = jnp.concatenate([p_hi, p_lo], axis=0)

    def w_term(k, span):
        t = dot(p2, m2[k, :, span])
        return t[:rank] + t[rank:]

    order = list(range(1, n_sh)) + [0]
    for ch, span in enumerate(spans):
        for i in order:
            o = at_sh(i)
            w_a[o, :, span] = w_term(2 * o + oc, span)
            send(w_a.at[o, :, span], w_b.at[o, :, span], c_s.at[ch, i], c_r.at[ch, o], (sib, s))
        if ch == 0:
            padded = jnp.concatenate([pt, jnp.zeros((128 - rank, n_rows), F32)], axis=0)
            gbuf[s] = dot(pt, padded, NT, HIGH)
            for i in range(1, n_sh):
                send(gbuf.at[s], gbuf.at[s], g_s.at[i], g_r.at[s], (d, at_sh(i)))
        for i in order:
            o = at_sh(i)
            own = w_term(2 * o + c, span)
            arrived(w_b.at[o, :, span], c_s.at[ch, i], c_r.at[ch, o])
            if i == 0:
                w_r[s, :, span] = own + w_b[s, :, span]
            else:
                w_c[o, :, span] = own + w_b[o, :, span]
                send(
                    w_c.at[o, :, span], w_r.at[s, :, span], w_s.at[ch, i], w_rs.at[ch, s], (d, at_sh(i))
                )

    for i in range(1, n_sh):
        o = at_sh(i)
        arrived(gbuf.at[o], g_s.at[i], g_r.at[o])
    gram = gbuf[0]
    for k in range(1, n_sh):
        gram = gram + gbuf[k]
    linv = inverse_factor(gram)
    p_hat_t = dot(linv, pt, NN, HIGH)
    three = jnp.concatenate([p_hat_t, p_hat_t, p_hat_t], axis=0)
    rounded = three.astype(BF16).astype(F32)
    row = lax.broadcasted_iota(jnp.int32, three.shape, 0)
    ph3 = jnp.where(row < 2 * rank, rounded, three - rounded).T.astype(BF16)

    def over_shards(ch, span):
        for i in range(1, n_sh):
            o = at_sh(i)
            arrived(w_r.at[o, :, span], w_s.at[ch, i], w_rs.at[ch, o])
        r = w_r[0, :, span]
        for k in range(1, n_sh):
            r = r + w_r[k, :, span]
        if split_z:
            for k in range(nz):
                r_buf[k, :, span] = r[k * zrows : (k + 1) * zrows]
            z_r[z, :, span] = r_buf[z, :, span]
        else:
            z_r[z, :, span] = r
        for i in range(1, nz):
            o = at_z(i)
            src = r_buf.at[o, :, span] if split_z else z_r.at[z, :, span]
            send(src, z_r.at[z, :, span], zr_s.at[ch, i], zr_r.at[ch, z], (2 * o + c, s))

    def over_z(ch, span):
        for i in range(1, nz):
            o = at_z(i)
            arrived(z_r.at[o, :, span], zr_s.at[ch, i], zr_r.at[ch, o])
        r = z_r[0, :, span]
        for k in range(1, nz):
            r = r + z_r[k, :, span]
        if split_z:
            z_full[z, :, span] = r
            part = z_full.at[z, :, span]
            for i in range(1, nz):
                send(part, part, za_s.at[ch, i], za_r.at[ch, z], (2 * at_z(i) + c, s))
        else:
            z_full[0, :, span] = r

    def share_out(ch, span):
        r = z_full[0, :, span]
        if split_z:
            for i in range(1, nz):
                o = at_z(i)
                arrived(z_full.at[o, :, span], za_s.at[ch, i], za_r.at[ch, o])
            r = jnp.concatenate([z_full[k, :, span] for k in range(nz)], axis=0)
        y_all[mine, :, span] = dot(linv, r, NN, HIGH)
        part = y_all.at[mine, :, span]
        for i in range(1, n_sh):
            send(part, part, y_s.at[ch, i], y_r.at[ch, s], (d, at_sh(i)))
        send(part, part, yc_s.at[ch, 0], yc_r.at[ch, s], (sib, s))

    for step in range(n_ch + 2):
        if step < n_ch:
            over_shards(step, spans[step])
        if 0 <= step - 1 < n_ch:
            over_z(step - 1, spans[step - 1])
        if 0 <= step - 2 < n_ch:
            share_out(step - 2, spans[step - 2])

    stores = []

    def finish(k, ch):
        lo_lane, hi_lane = chunks[ch]
        hi, lo = halves(y_all[k, :, spans[ch]])
        mf[k, :, spans[ch]] = mf[k, :, spans[ch]] - dot(ph3, jnp.concatenate([hi, lo, hi], axis=0))
        if aligned:
            columns = pl.ds(pl.multiple_of(k * width + lo_lane, 128), hi_lane - lo_lane)
            copy = pltpu.make_async_copy(
                mf.at[k, :, spans[ch]], out_hbm.at[0, :, columns], out_sem.at[len(stores)]
            )
            copy.start()
            stores.append(copy)

    for ch, span in enumerate(spans):
        finish(mine, ch)
        arrived(y_all.at[other, :, span], yc_s.at[ch, 0], yc_r.at[ch, s])
        finish(other, ch)
    late = []
    for h in range(2):
        if aligned:
            target = qnew_hbm.at[:, h * width : (h + 1) * width]
            copy = pltpu.make_async_copy(y_all.at[2 * s + h], target, qn_sem.at[h])
            copy.start()
            late.append(copy)
        else:
            qn_v[:, h * width : (h + 1) * width] = y_all[2 * s + h]
    for ch, span in enumerate(spans):
        for i in range(1, n_sh):
            o = at_sh(i)
            part = y_all.at[2 * o + c, :, span]
            arrived(part, y_s.at[ch, i], y_r.at[ch, o])
            send(part, part, yc_s.at[ch, i], yc_r.at[ch, o], (sib, s))
        for i in range(1, n_sh):
            finish(2 * at_sh(i) + c, ch)
        for i in range(1, n_sh):
            o = at_sh(i)
            arrived(y_all.at[2 * o + oc, :, span], yc_s.at[ch, i], yc_r.at[ch, o])
            finish(2 * o + oc, ch)
    if not aligned:
        for k in range(pieces):
            out_v[:, k * width : (k + 1) * width] = mf[k]
        for src, dst, sem in ((out_v, out_hbm.at[0], out_sem.at[0]), (qn_v, qnew_hbm, qn_sem.at[0])):
            copy = pltpu.make_async_copy(src, dst, sem)
            copy.start()
            late.append(copy)
    for copy in sends:
        copy.wait_send()
    for copy in stores + late:
        copy.wait()


def place(out_from, q_from, out_to, q_to, sems):
    n_rows = out_from.shape[1]
    step = n_rows // PLACE_PARTS
    copies = [pltpu.make_async_copy(q_from, q_to, sems.at[PLACE_PARTS])]
    for i in range(PLACE_PARTS):
        rows = pl.ds(i * step, step)
        copies.append(pltpu.make_async_copy(out_from.at[0, rows], out_to.at[0, rows], sems.at[i]))
    for copy in copies:
        copy.start()
    for copy in copies:
        copy.wait()


def per_device(n_dp, n_sh, grads, errors, q_prev):
    _, n_rows, full = grads.shape
    share, rank = q_prev.shape
    width = share // 2
    nz = n_dp // 2
    split_z = rank % (8 * nz) == 0
    zrows = rank // nz if split_z else rank
    aligned = width % 128 == 0
    pieces = 2 * n_sh
    dims = (n_dp, n_sh, nz, zrows, split_z, aligned, width)
    chunks = ((0, width),)
    if aligned and width >= N_CHUNKS * 128:
        tiles = width // 128
        edges = [-(-tiles * i // N_CHUNKS) * 128 for i in range(N_CHUNKS + 1)]
        chunks = tuple(zip(edges[:-1], edges[1:]))
    vm = pltpu.VMEM
    dma = pltpu.SemaphoreType.DMA
    small = (8, 128)
    scratch = [
        vm((n_rows, full), BF16),
        vm((n_rows, full), F32),
        vm(small if aligned else (rank, share), F32),
        vm((pieces, 2 * n_rows, width), BF16),
        vm((pieces, n_rows, width), F32),
        vm((pieces, rank, width), F32),
        vm((n_dp, rank // 2, 2 * n_rows), F32),
        vm((n_sh, rank, 128), F32),
        vm((n_sh, rank, width), F32),
        vm((n_sh, rank, width), F32),
        vm((n_sh, rank, width), F32),
        vm((n_sh, rank, width), F32),
        vm((nz, zrows, width) if split_z else small, F32),
        vm((nz, zrows, width), F32),
        vm((nz, zrows, width) if split_z else (1, rank, width), F32),
        vm((pieces, rank, width), F32),
        vm(small if aligned else (n_rows, full), F32),
        vm(small if aligned else (rank, share), F32),
        dma((4,)),
    ]
    n_ch = len(chunks)
    per_chunk = [(n_ch, n_sh)] * 2 + [(n_dp,), (n_sh,)] + [(n_ch, n_sh)] * 2 + [(n_ch, nz)] * 2 + [(n_ch, n_sh)] * 2
    for shape in per_chunk:
        scratch += [dma(shape), dma(shape)]
    scratch += [dma((n_ch * pieces,)), dma((2,))]
    shapes = (
        jax.ShapeDtypeStruct((1, n_rows, full), F32),
        jax.ShapeDtypeStruct((rank, share), F32),
    )
    hbm = pl.BlockSpec(memory_space=pl.ANY)
    out, q_new = pl.pallas_call(
        functools.partial(kernel, dims, chunks),
        out_shape=shapes,
        in_specs=[hbm, hbm, hbm],
        out_specs=(hbm, hbm),
        scratch_shapes=scratch,
        compiler_params=pltpu.CompilerParams(
            collective_id=0, has_side_effects=True, vmem_limit_bytes=62 * 1024 * 1024
        ),
        cost_estimate=pl.CostEstimate(
            flops=18 * n_rows * full * rank, bytes_accessed=10 * n_rows * full, transcendentals=0
        ),
    )(grads, errors, q_prev.T)
    out, q_new = pl.pallas_call(
        place,
        out_shape=shapes,
        in_specs=[hbm, hbm],
        out_specs=(hbm, hbm),
        scratch_shapes=[dma((PLACE_PARTS + 1,))],
        compiler_params=pltpu.CompilerParams(vmem_limit_bytes=62 * 1024 * 1024),
    )(out, q_new)
    return out, q_new.T


def solution(mesh):
    in_specs = (P("dp", "shard", None), P("dp", "shard", None), P("shard", None))
    out_specs = (P("dp", "shard", None), P("shard", None))
    return jax.shard_map(
        functools.partial(per_device, mesh.shape["dp"], mesh.shape["shard"]),
        mesh=mesh, in_specs=in_specs, out_specs=out_specs, check_vma=False,
    )
```

time: 48.8 us -> 107 us (2.19)
  Pallas kernels: 44 us -> 106 us
  local copies, waits for them, and re-layouts: 3.59 us -> 0 us
    pallas_call x1 -> x2, Pallas kernels: 44 us -> 106 us  [the longest x1 63.7 us: per_device(): pl.pallas_call(place, out_shape=shapes, in_specs=[hbm, hbm], out_specs=(h...]
    unnamed x4 -> x0, local copies, waits for them, and re-layouts: 3.59 us -> none
where the time goes in v3:
time: 107 us
  Pallas kernels  106 us (99%)
    pallas_call x1, Pallas kernels, per_device(): pl.pallas_call(place, out_shape=shapes, in_specs=[hbm, hbm], out_specs=(h...  63.7 us
    pallas_call x1, Pallas kernels, per_device(): pl.pallas_call(functools.partial(kernel, dims, chunks), out_shape=shapes,...  42.5 us

profile of v3, /device:TPU:0, one launch (start us, length us, event | category | flops | bytes accessed | tf_op | source)
XLA Modules:
  0.0 106.9 jit_solution(2352650073800459644)
XLA Ops:
  0.6 42.5 %shard_map.50 = (f32[1,64,7168]{2,1,0:T(8,128)}, f32[32,1792]{1,0:T(8,128)}) custom-call(bf16[1,64,7168]{2,1,0:T(8,128)(2,1)} %g_hbm.1, f32[1,64,7168]{2,1,0:T(8,128)} %e_hbm.1, f32[32,1792]{1,0:T(8,128)} %bitcast.2), custom_call_target="tpu_custom_call" | custom-call | flops 264241152 | bytes 4587520 | tf_op jit(solution)/shard_map/pallas_call | solution.py:382
  43.2 63.7 %shard_map.51 = (f32[1,64,7168]{2,1,0:T(8,128)}, f32[32,1792]{1,0:T(8,128)}) custom-call(f32[1,64,7168]{2,1,0:T(8,128)} %get-tuple-element.6.out_from, f32[32,1792]{1,0:T(8,128)} %get-tuple-element.7.q_from), custom_call_target="tpu_custom_call" | custom-call | tf_op jit(solution)/shard_map/pallas_call | solution.py:395

commit v4 on v3

--- a/solution.py
+++ b/solution.py
@@ -1,4 +1,5 @@
 import functools
+import math
 
 import jax
 import jax.numpy as jnp
@@ -51,7 +52,7 @@
     in_sem, q_s, q_r, qf_s, qf_r, p_s, p_r, g_s, g_r, c_s, c_r, w_s, w_rs, zr_s, zr_r, za_s, za_r,
     y_s, y_r, yc_s, yc_r, out_sem, qn_sem,
 ):
-    n_dp, n_sh, nz, zrows, split_z, aligned, width = dims
+    n_dp, n_sh, side, nz, zrows, split_z, aligned, width = dims
     spans = [pl.ds(lo, hi - lo) for lo, hi in chunks]
     n_ch = len(chunks)
     rank = q_hbm.shape[0]
@@ -83,8 +84,11 @@
     def at_dp(i):
         return lax.rem(d + i, n_dp)
 
-    def at_sh(i):
-        return lax.rem(s + i, n_sh)
+    def at_sh(i, core=c):
+        first, second = i % side, i // side
+        across = first + core * (second - first)
+        down = second + core * (first - second)
+        return lax.rem(s // side + down, side) * side + lax.rem(s % side + across, side)
 
     def at_z(i):
         return lax.rem(z + i, nz)
@@ -147,7 +151,7 @@
         for i in range(1, n_sh):
             acc = acc + left_term(2 * at_sh(i) + c, span)
         for i in range(1, n_sh):
-            o = at_sh(i)
+            o = at_sh(i, oc)
             arrived(q_all.at[2 * o + oc, :, span], qf_s.at[ch, i], qf_r.at[ch, o])
             acc = acc + left_term(2 * o + oc, span)
     acc = acc[:rank] + acc[rank:]
@@ -178,7 +182,7 @@
     order = list(range(1, n_sh)) + [0]
     for ch, span in enumerate(spans):
         for i in order:
-            o = at_sh(i)
+            o = at_sh(i, oc)
             w_a[o, :, span] = w_term(2 * o + oc, span)
             send(w_a.at[o, :, span], w_b.at[o, :, span], c_s.at[ch, i], c_r.at[ch, o], (sib, s))
         if ch == 0:
@@ -301,7 +305,7 @@
         for i in range(1, n_sh):
             finish(2 * at_sh(i) + c, ch)
         for i in range(1, n_sh):
-            o = at_sh(i)
+            o = at_sh(i, oc)
             arrived(y_all.at[2 * o + oc, :, span], yc_s.at[ch, i], yc_r.at[ch, o])
             finish(2 * o + oc, ch)
     if not aligned:
@@ -317,17 +321,22 @@
         copy.wait()
 
 
-def place(out_from, q_from, out_to, q_to, sems):
+def place(out_from, q_from, out_to, q_to, out_v, q_v, in_sems, out_sems):
     n_rows = out_from.shape[1]
     step = n_rows // PLACE_PARTS
-    copies = [pltpu.make_async_copy(q_from, q_to, sems.at[PLACE_PARTS])]
+    pairs = [(q_from, q_v, q_to)]
     for i in range(PLACE_PARTS):
         rows = pl.ds(i * step, step)
-        copies.append(pltpu.make_async_copy(out_from.at[0, rows], out_to.at[0, rows], sems.at[i]))
-    for copy in copies:
-        copy.start()
-    for copy in copies:
-        copy.wait()
+        pairs.append((out_from.at[0, rows], out_v.at[rows], out_to.at[0, rows]))
+    loads = [pltpu.make_async_copy(src, mid, in_sems.at[i]) for i, (src, mid, _) in enumerate(pairs)]
+    stores = [pltpu.make_async_copy(mid, dst, out_sems.at[i]) for i, (_, mid, dst) in enumerate(pairs)]
+    for load in loads:
+        load.start()
+    for load, store in zip(loads, stores):
+        load.wait()
+        store.start()
+    for store in stores:
+        store.wait()
 
 
 def per_device(n_dp, n_sh, grads, errors, q_prev):
@@ -339,7 +348,7 @@
     zrows = rank // nz if split_z else rank
     aligned = width % 128 == 0
     pieces = 2 * n_sh
-    dims = (n_dp, n_sh, nz, zrows, split_z, aligned, width)
+    dims = (n_dp, n_sh, math.isqrt(n_sh), nz, zrows, split_z, aligned, width)
     chunks = ((0, width),)
     if aligned and width >= N_CHUNKS * 128:
         tiles = width // 128
@@ -397,7 +406,9 @@
         out_shape=shapes,
         in_specs=[hbm, hbm],
         out_specs=(hbm, hbm),
-        scratch_shapes=[dma((PLACE_PARTS + 1,))],
+        scratch_shapes=[
+            vm((n_rows, full), F32), vm((rank, share), F32), dma((PLACE_PARTS + 1,)), dma((PLACE_PARTS + 1,)),
+        ],
         compiler_params=pltpu.CompilerParams(vmem_limit_bytes=62 * 1024 * 1024),
     )(out, q_new)
     return out, q_new.T

time: 107 us -> 46 us (0.43)
  Pallas kernels: 106 us -> 45.2 us
    pallas_call x1, Pallas kernels: 63.7 us -> 2.45 us  [per_device(): pl.pallas_call(place, out_shape=shapes, in_specs=[hbm, hbm], out_specs=(h...]
where the time goes in v4:
time: 46 us; the launch traced here: 45.8 us
  Pallas kernels  45.2 us (98%)
  between operations  0.64 us (1%)
    pallas_call x1, Pallas kernels, per_device(): pl.pallas_call(functools.partial(kernel, dims, chunks), out_shape=shapes,...  42.7 us
    pallas_call x1, Pallas kernels, per_device(): pl.pallas_call(place, out_shape=shapes, in_specs=[hbm, hbm], out_specs=(h...  2.45 us

profile of v4, /device:TPU:0, one launch (start us, length us, event | category | flops | bytes accessed | tf_op | source)
XLA Modules:
  0.0 45.8 jit_solution(11717668284424137565)
XLA Ops:
  0.6 42.7 %shard_map.50 = (f32[1,64,7168]{2,1,0:T(8,128)}, f32[32,1792]{1,0:T(8,128)}) custom-call(bf16[1,64,7168]{2,1,0:T(8,128)(2,1)} %g_hbm.1, f32[1,64,7168]{2,1,0:T(8,128)} %e_hbm.1, f32[32,1792]{1,0:T(8,128)} %bitcast.2), custom_call_target="tpu_custom_call" | custom-call | flops 264241152 | bytes 4587520 | tf_op jit(solution)/shard_map/pallas_call | solution.py:391
  43.4 2.4 %shard_map.51 = (f32[1,64,7168]{2,1,0:T(8,128)}, f32[32,1792]{1,0:T(8,128)}) custom-call(f32[1,64,7168]{2,1,0:T(8,128)} %get-tuple-element.6.out_from, f32[32,1792]{1,0:T(8,128)} %get-tuple-element.7.q_from), custom_call_target="tpu_custom_call" | custom-call | tf_op jit(solution)/shard_map/pallas_call | solution.py:404

commit v5 on v4

--- a/solution.py
+++ b/solution.py
@@ -48,8 +48,8 @@
 
 def kernel(
     dims, chunks, g_hbm, e_hbm, q_hbm, out_hbm, qnew_hbm,
-    g_v, e_v, q_v, m2, mf, q_all, pbuf, gbuf, w_a, w_b, w_c, w_r, r_buf, z_r, z_full, y_all, out_v, qn_v,
-    in_sem, q_s, q_r, qf_s, qf_r, p_s, p_r, g_s, g_r, c_s, c_r, w_s, w_rs, zr_s, zr_r, za_s, za_r,
+    g_v, e_v, q_v, m2, mf, mx, q_all, pbuf, gbuf, w_c, w_r, r_buf, z_r, z_full, y_all, out_v, qn_v,
+    in_sem, q_s, q_r, p_s, p_r, g_s, g_r, m_s, m_r, w_s, w_rs, zr_s, zr_r, za_s, za_r,
     y_s, y_r, yc_s, yc_r, out_sem, qn_sem,
 ):
     n_dp, n_sh, side, nz, zrows, split_z, aligned, width = dims
@@ -131,31 +131,33 @@
     load_e.wait()
     for k in range(pieces):
         cols = slice(k * width, (k + 1) * width)
-        m = g_v[:, cols].astype(F32) + e_v[:, cols]
-        hi, lo = halves(m)
-        mf[k] = m
-        m2[k, : m.shape[0]] = hi
-        m2[k, m.shape[0] :] = lo
-
-    def left_term(k, span):
-        hi, lo = halves(q_all[k, :, span])
-        return dot(jnp.concatenate([hi, lo], axis=0), m2[k, :, span], NT)
-
-    acc = left_term(2 * s, pl.ds(0, width)) + left_term(2 * s + 1, pl.ds(0, width))
+        mf[k] = g_v[:, cols].astype(F32) + e_v[:, cols]
+
+    swaps = []
+    for i in range(n_sh):
+        o = at_sh(i)
+        swap = remote(mf.at[2 * o + oc], mx.at[o], m_s.at[i], m_r.at[o], (sib, s))
+        swap.start()
+        swaps.append(swap)
+    n_rows = mf.shape[1]
+    for i in range(n_sh):
+        o = at_sh(i)
+        arrived(mx.at[o], m_s.at[i], m_r.at[o])
+        hi, lo = halves(mf[2 * o + c] + mx[o])
+        m2[o, :n_rows] = hi
+        m2[o, n_rows:] = lo
+
+    def left_term(o, span):
+        hi, lo = halves(q_all[2 * o + c, :, span])
+        return dot(jnp.concatenate([hi, lo], axis=0), m2[o, :, span], NT)
+
+    acc = left_term(s, pl.ds(0, width))
     for ch, span in enumerate(spans):
         for i in range(1, n_sh):
             o = at_sh(i)
-            part = q_all.at[2 * o + c, :, span]
-            arrived(part, q_s.at[ch, i], q_r.at[ch, o])
-            send(part, part, qf_s.at[ch, i], qf_r.at[ch, o], (sib, s))
-        for i in range(1, n_sh):
-            acc = acc + left_term(2 * at_sh(i) + c, span)
-        for i in range(1, n_sh):
-            o = at_sh(i, oc)
-            arrived(q_all.at[2 * o + oc, :, span], qf_s.at[ch, i], qf_r.at[ch, o])
-            acc = acc + left_term(2 * o + oc, span)
+            arrived(q_all.at[2 * o + c, :, span], q_s.at[ch, i], q_r.at[ch, o])
+            acc = acc + left_term(o, span)
     acc = acc[:rank] + acc[rank:]
-    n_rows = mf.shape[1]
     part = acc[:, :n_rows] + acc[:, n_rows:]
     half = rank // 2
 
@@ -175,32 +177,24 @@
     p_hi, p_lo = halves(twice)
     p2 = jnp.concatenate([p_hi, p_lo], axis=0)
 
-    def w_term(k, span):
-        t = dot(p2, m2[k, :, span])
+    def w_term(o, span):
+        t = dot(p2, m2[o, :, span])
         return t[:rank] + t[rank:]
 
-    order = list(range(1, n_sh)) + [0]
     for ch, span in enumerate(spans):
-        for i in order:
-            o = at_sh(i, oc)
-            w_a[o, :, span] = w_term(2 * o + oc, span)
-            send(w_a.at[o, :, span], w_b.at[o, :, span], c_s.at[ch, i], c_r.at[ch, o], (sib, s))
+        for i in range(1, n_sh):
+            o = at_sh(i)
+            w_c[o, :, span] = w_term(o, span)
+            send(w_c.at[o, :, span], w_r.at[s, :, span], w_s.at[ch, i], w_rs.at[ch, s], (d, at_sh(i)))
         if ch == 0:
             padded = jnp.concatenate([pt, jnp.zeros((128 - rank, n_rows), F32)], axis=0)
             gbuf[s] = dot(pt, padded, NT, HIGH)
             for i in range(1, n_sh):
                 send(gbuf.at[s], gbuf.at[s], g_s.at[i], g_r.at[s], (d, at_sh(i)))
-        for i in order:
-            o = at_sh(i)
-            own = w_term(2 * o + c, span)
-            arrived(w_b.at[o, :, span], c_s.at[ch, i], c_r.at[ch, o])
-            if i == 0:
-                w_r[s, :, span] = own + w_b[s, :, span]
-            else:
-                w_c[o, :, span] = own + w_b[o, :, span]
-                send(
-                    w_c.at[o, :, span], w_r.at[s, :, span], w_s.at[ch, i], w_rs.at[ch, s], (d, at_sh(i))
-                )
+    for span in spans:
+        w_r[s, :, span] = w_term(s, span)
+    for swap in swaps:
+        swap.wait_send()
 
     for i in range(1, n_sh):
         o = at_sh(i)
@@ -214,6 +208,11 @@
     rounded = three.astype(BF16).astype(F32)
     row = lax.broadcasted_iota(jnp.int32, three.shape, 0)
     ph3 = jnp.where(row < 2 * rank, rounded, three - rounded).T.astype(BF16)
+
+    l3 = jnp.concatenate([linv, linv, linv], axis=1)
+    l_rounded = l3.astype(BF16).astype(F32)
+    lane = lax.broadcasted_iota(jnp.int32, l3.shape, 1)
+    l3 = jnp.where(lane < 2 * rank, l_rounded, l3 - l_rounded).astype(BF16)
 
     def over_shards(ch, span):
         for i in range(1, n_sh):
@@ -255,7 +254,8 @@
                 o = at_z(i)
                 arrived(z_full.at[o, :, span], za_s.at[ch, i], za_r.at[ch, o])
             r = jnp.concatenate([z_full[k, :, span] for k in range(nz)], axis=0)
-        y_all[mine, :, span] = dot(linv, r, NN, HIGH)
+        hi, lo = halves(r)
+        y_all[mine, :, span] = dot(l3, jnp.concatenate([hi, lo, hi], axis=0))
         part = y_all.at[mine, :, span]
         for i in range(1, n_sh):
             send(part, part, y_s.at[ch, i], y_r.at[ch, s], (d, at_sh(i)))
@@ -361,13 +361,12 @@
         vm((n_rows, full), BF16),
         vm((n_rows, full), F32),
         vm(small if aligned else (rank, share), F32),
-        vm((pieces, 2 * n_rows, width), BF16),
+        vm((n_sh, 2 * n_rows, width), BF16),
         vm((pieces, n_rows, width), F32),
+        vm((n_sh, n_rows, width), F32),
         vm((pieces, rank, width), F32),
         vm((n_dp, rank // 2, 2 * n_rows), F32),
         vm((n_sh, rank, 128), F32),
-        vm((n_sh, rank, width), F32),
-        vm((n_sh, rank, width), F32),
         vm((n_sh, rank, width), F32),
         vm((n_sh, rank, width), F32),
         vm((nz, zrows, width) if split_z else small, F32),
@@ -379,7 +378,7 @@
         dma((4,)),
     ]
     n_ch = len(chunks)
-    per_chunk = [(n_ch, n_sh)] * 2 + [(n_dp,), (n_sh,)] + [(n_ch, n_sh)] * 2 + [(n_ch, nz)] * 2 + [(n_ch, n_sh)] * 2
+    per_chunk = [(n_ch, n_sh), (n_dp,), (n_sh,), (n_sh,), (n_ch, n_sh)] + [(n_ch, nz)] * 2 + [(n_ch, n_sh)] * 2
     for shape in per_chunk:
         scratch += [dma(shape), dma(shape)]
     scratch += [dma((n_ch * pieces,)), dma((2,))]

time: 46 us -> 44.7 us (0.972)
  Pallas kernels: 45.2 us -> 43.9 us
    pallas_call x1, Pallas kernels: 42.7 us -> 41.4 us  [per_device(): pl.pallas_call(functools.partial(kernel, dims, chunks), out_shape=shapes,...]
where the time goes in v5:
time: 44.7 us; the launch traced here: 44.5 us
  Pallas kernels  43.9 us (98%)
  between operations  0.64 us (1%)
    pallas_call x1, Pallas kernels, per_device(): pl.pallas_call(functools.partial(kernel, dims, chunks), out_shape=shapes,...  41.4 us
    pallas_call x1, Pallas kernels, per_device(): pl.pallas_call(place, out_shape=shapes, in_specs=[hbm, hbm], out_specs=(h...  2.45 us

profile of v5, /device:TPU:0, one launch (start us, length us, event | category | flops | bytes accessed | tf_op | source)
XLA Modules:
  0.0 44.5 jit_solution(9234721480830181656)
XLA Ops:
  0.6 41.4 %shard_map.50 = (f32[1,64,7168]{2,1,0:T(8,128)}, f32[32,1792]{1,0:T(8,128)}) custom-call(bf16[1,64,7168]{2,1,0:T(8,128)(2,1)} %g_hbm.1, f32[1,64,7168]{2,1,0:T(8,128)} %e_hbm.1, f32[32,1792]{1,0:T(8,128)} %bitcast.2), custom_call_target="tpu_custom_call" | custom-call | flops 264241152 | bytes 4587520 | tf_op jit(solution)/shard_map/pallas_call | solution.py:390
  42.1 2.4 %shard_map.51 = (f32[1,64,7168]{2,1,0:T(8,128)}, f32[32,1792]{1,0:T(8,128)}) custom-call(f32[1,64,7168]{2,1,0:T(8,128)} %get-tuple-element.6.out_from, f32[32,1792]{1,0:T(8,128)} %get-tuple-element.7.q_from), custom_call_target="tpu_custom_call" | custom-call | tf_op jit(solution)/shard_map/pallas_call | solution.py:403

commit v6 on v5

--- a/solution.py
+++ b/solution.py
@@ -48,7 +48,7 @@
 
 def kernel(
     dims, chunks, g_hbm, e_hbm, q_hbm, out_hbm, qnew_hbm,
-    g_v, e_v, q_v, m2, mf, mx, q_all, pbuf, gbuf, w_c, w_r, r_buf, z_r, z_full, y_all, out_v, qn_v,
+    g_v, e_v, q_v, m2, mf, mx, q_all, pbuf, gbuf, w_c, w_r, w_t, r_buf, z_r, z_full, y_all, out_v, qn_v,
     in_sem, q_s, q_r, p_s, p_r, g_s, g_r, m_s, m_r, w_s, w_rs, zr_s, zr_r, za_s, za_r,
     y_s, y_r, yc_s, yc_r, out_sem, qn_sem,
 ):
@@ -90,6 +90,9 @@
         down = second + core * (first - second)
         return lax.rem(s // side + down, side) * side + lax.rem(s % side + across, side)
 
+    relay = side == 2 and n_ch == 2
+    near, far, diag = at_sh(1), at_sh(2), at_sh(3)
+
     def at_z(i):
         return lax.rem(z + i, nz)
 
@@ -122,10 +125,26 @@
 
     mine = 2 * s + c
     other = 2 * s + oc
-    for ch, span in enumerate(spans):
-        part = q_all.at[mine, :, span]
-        for i in range(1, n_sh):
-            send(part, part, q_s.at[ch, i], q_r.at[ch, s], (d, at_sh(i)))
+    def spread(buf, ch, sem_s, sem_r, peer, i):
+        part = buf.at[mine, :, spans[ch]]
+        send(part, part, sem_s.at[ch, i], sem_r.at[ch, s], (d, peer))
+
+    def pass_on(buf, ch, sem_s, sem_r, owner, peer):
+        part = buf.at[2 * owner + c, :, spans[ch]]
+        send(part, part, sem_s.at[ch, 3], sem_r.at[ch, owner], (d, peer))
+
+    def landed(buf, ch, sem_s, sem_r, owner):
+        arrived(buf.at[2 * owner + c, :, spans[ch]], sem_s.at[ch, 1], sem_r.at[ch, owner])
+
+    if relay:
+        spread(q_all, 0, q_s, q_r, near, 1)
+        spread(q_all, 1, q_s, q_r, far, 2)
+        spread(q_all, 1, q_s, q_r, near, 1)
+        spread(q_all, 0, q_s, q_r, far, 2)
+    else:
+        for ch in range(n_ch):
+            for i in range(1, n_sh):
+                spread(q_all, ch, q_s, q_r, at_sh(i), i)
 
     load_g.wait()
     load_e.wait()
@@ -152,11 +171,20 @@
         return dot(jnp.concatenate([hi, lo], axis=0), m2[o, :, span], NT)
 
     acc = left_term(s, pl.ds(0, width))
-    for ch, span in enumerate(spans):
-        for i in range(1, n_sh):
-            o = at_sh(i)
-            arrived(q_all.at[2 * o + c, :, span], q_s.at[ch, i], q_r.at[ch, o])
-            acc = acc + left_term(o, span)
+    if relay:
+        landed(q_all, 0, q_s, q_r, near)
+        pass_on(q_all, 0, q_s, q_r, near, far)
+        landed(q_all, 1, q_s, q_r, far)
+        pass_on(q_all, 1, q_s, q_r, far, near)
+        acc = acc + left_term(near, spans[0]) + left_term(far, spans[1])
+        for ch, owner in ((1, near), (0, far), (0, diag), (1, diag)):
+            landed(q_all, ch, q_s, q_r, owner)
+            acc = acc + left_term(owner, spans[ch])
+    else:
+        for ch, span in enumerate(spans):
+            for i in range(1, n_sh):
+                landed(q_all, ch, q_s, q_r, at_sh(i))
+                acc = acc + left_term(at_sh(i), span)
     acc = acc[:rank] + acc[rank:]
     part = acc[:, :n_rows] + acc[:, n_rows:]
     half = rank // 2
@@ -181,16 +209,40 @@
         t = dot(p2, m2[o, :, span])
         return t[:rank] + t[rank:]
 
-    for ch, span in enumerate(spans):
+    def gram_terms():
+        padded = jnp.concatenate([pt, jnp.zeros((128 - rank, n_rows), F32)], axis=0)
+        gbuf[s] = dot(pt, padded, NT, HIGH)
         for i in range(1, n_sh):
-            o = at_sh(i)
-            w_c[o, :, span] = w_term(o, span)
-            send(w_c.at[o, :, span], w_r.at[s, :, span], w_s.at[ch, i], w_rs.at[ch, s], (d, at_sh(i)))
-        if ch == 0:
-            padded = jnp.concatenate([pt, jnp.zeros((128 - rank, n_rows), F32)], axis=0)
-            gbuf[s] = dot(pt, padded, NT, HIGH)
-            for i in range(1, n_sh):
-                send(gbuf.at[s], gbuf.at[s], g_s.at[i], g_r.at[s], (d, at_sh(i)))
+            send(gbuf.at[s], gbuf.at[s], g_s.at[i], g_r.at[s], (d, at_sh(i)))
+
+    def give(ch, peer, i):
+        span = spans[ch]
+        send(w_c.at[peer, :, span], w_r.at[s, :, span], w_s.at[ch, i], w_rs.at[ch, s], (d, peer))
+
+    if relay:
+        for ch, peer, slot in ((0, near, far), (1, far, near)):
+            span = spans[ch]
+            w_c[diag, :, span] = w_term(diag, span)
+            send(w_c.at[diag, :, span], w_t.at[:, span], w_s.at[ch, 3], w_rs.at[ch, slot + n_sh], (d, peer))
+        w_c[near, :, spans[0]] = w_term(near, spans[0])
+        give(0, near, 1)
+        w_c[far, :, spans[1]] = w_term(far, spans[1])
+        give(1, far, 2)
+        gram_terms()
+        for ch, peer, i in ((0, far, 2), (1, near, 1)):
+            span = spans[ch]
+            own = w_term(peer, span)
+            arrived(w_t.at[:, span], w_s.at[ch, 3], w_rs.at[ch, diag + n_sh])
+            w_c[peer, :, span] = own + w_t[:, span]
+            give(ch, peer, i)
+    else:
+        for ch, span in enumerate(spans):
+            for i in range(1, n_sh):
+                o = at_sh(i)
+                w_c[o, :, span] = w_term(o, span)
+                give(ch, o, i)
+            if ch == 0:
+                gram_terms()
     for span in spans:
         w_r[s, :, span] = w_term(s, span)
     for swap in swaps:
@@ -215,12 +267,11 @@
     l3 = jnp.where(lane < 2 * rank, l_rounded, l3 - l_rounded).astype(BF16)
 
     def over_shards(ch, span):
-        for i in range(1, n_sh):
-            o = at_sh(i)
-            arrived(w_r.at[o, :, span], w_s.at[ch, i], w_rs.at[ch, o])
-        r = w_r[0, :, span]
-        for k in range(1, n_sh):
-            r = r + w_r[k, :, span]
+        sources = [near, far] if relay else [at_sh(i) for i in range(1, n_sh)]
+        r = w_r[s, :, span]
+        for o in sources:
+            arrived(w_r.at[o, :, span], w_s.at[ch, 1], w_rs.at[ch, o])
+            r = r + w_r[o, :, span]
         if split_z:
             for k in range(nz):
                 r_buf[k, :, span] = r[k * zrows : (k + 1) * zrows]
@@ -257,8 +308,8 @@
         hi, lo = halves(r)
         y_all[mine, :, span] = dot(l3, jnp.concatenate([hi, lo, hi], axis=0))
         part = y_all.at[mine, :, span]
-        for i in range(1, n_sh):
-            send(part, part, y_s.at[ch, i], y_r.at[ch, s], (d, at_sh(i)))
+        for i in (1 + ch, 2 - ch) if relay else range(1, n_sh):
+            spread(y_all, ch, y_s, y_r, at_sh(i), i)
         send(part, part, yc_s.at[ch, 0], yc_r.at[ch, s], (sib, s))
 
     for step in range(n_ch + 2):
@@ -296,18 +347,37 @@
             late.append(copy)
         else:
             qn_v[:, h * width : (h + 1) * width] = y_all[2 * s + h]
-    for ch, span in enumerate(spans):
-        for i in range(1, n_sh):
-            o = at_sh(i)
-            part = y_all.at[2 * o + c, :, span]
-            arrived(part, y_s.at[ch, i], y_r.at[ch, o])
-            send(part, part, yc_s.at[ch, i], yc_r.at[ch, o], (sib, s))
-        for i in range(1, n_sh):
-            finish(2 * at_sh(i) + c, ch)
-        for i in range(1, n_sh):
-            o = at_sh(i, oc)
-            arrived(y_all.at[2 * o + oc, :, span], yc_s.at[ch, i], yc_r.at[ch, o])
-            finish(2 * o + oc, ch)
+    def hand_over(ch, owner, i):
+        part = y_all.at[2 * owner + c, :, spans[ch]]
+        send(part, part, yc_s.at[ch, i], yc_r.at[ch, owner], (sib, s))
+
+    def take(ch, owner):
+        arrived(y_all.at[2 * owner + oc, :, spans[ch]], yc_s.at[ch, 0], yc_r.at[ch, owner])
+        finish(2 * owner + oc, ch)
+
+    if relay:
+        first = ((0, near, far, 1), (1, far, near, 2))
+        rest = ((0, far, 2), (1, near, 1), (0, diag, 3), (1, diag, 3))
+        for ch, owner, peer, i in first:
+            landed(y_all, ch, y_s, y_r, owner)
+            pass_on(y_all, ch, y_s, y_r, owner, peer)
+            hand_over(ch, owner, i)
+            finish(2 * owner + c, ch)
+        for ch, owner, i in rest:
+            landed(y_all, ch, y_s, y_r, owner)
+            hand_over(ch, owner, i)
+            finish(2 * owner + c, ch)
+        for ch, owner in ((0, far), (1, near), (0, near), (1, far), (0, diag), (1, diag)):
+            take(ch, owner)
+    else:
+        for ch in range(n_ch):
+            for i in range(1, n_sh):
+                landed(y_all, ch, y_s, y_r, at_sh(i))
+                hand_over(ch, at_sh(i), i)
+            for i in range(1, n_sh):
+                finish(2 * at_sh(i) + c, ch)
+            for i in range(1, n_sh):
+                take(ch, at_sh(i, oc))
     if not aligned:
         for k in range(pieces):
             out_v[:, k * width : (k + 1) * width] = mf[k]
@@ -369,6 +439,7 @@
         vm((n_sh, rank, 128), F32),
         vm((n_sh, rank, width), F32),
         vm((n_sh, rank, width), F32),
+        vm((rank, width), F32),
         vm((nz, zrows, width) if split_z else small, F32),
         vm((nz, zrows, width), F32),
         vm((nz, zrows, width) if split_z else (1, rank, width), F32),
@@ -379,6 +450,7 @@
     ]
     n_ch = len(chunks)
     per_chunk = [(n_ch, n_sh), (n_dp,), (n_sh,), (n_sh,), (n_ch, n_sh)] + [(n_ch, nz)] * 2 + [(n_ch, n_sh)] * 2
+    per_chunk[4] = (n_ch, 2 * n_sh)
     for shape in per_chunk:
         scratch += [dma(shape), dma(shape)]
     scratch += [dma((n_ch * pieces,)), dma((2,))]

time: 44.7 us -> 45.6 us (1.020)
  Pallas kernels: 43.9 us -> 44.8 us
    pallas_call x1, Pallas kernels: 41.4 us -> 42.3 us  [per_device(): pl.pallas_call(functools.partial(kernel, dims, chunks), out_shape=shapes,...]
where the time goes in v6:
time: 45.6 us; the launch traced here: 45.4 us
  Pallas kernels  44.8 us (98%)
  between operations  0.64 us (1%)
    pallas_call x1, Pallas kernels, per_device(): pl.pallas_call(functools.partial(kernel, dims, chunks), out_shape=shapes,...  42.3 us
    pallas_call x1, Pallas kernels, per_device(): pl.pallas_call(place, out_shape=shapes, in_specs=[hbm, hbm], out_specs=(h...  2.45 us

profile of v6, /device:TPU:0, one launch (start us, length us, event | category | flops | bytes accessed | tf_op | source)
XLA Modules:
  0.0 45.4 jit_solution(5871793451956418351)
XLA Ops:
  0.6 42.3 %shard_map.50 = (f32[1,64,7168]{2,1,0:T(8,128)}, f32[32,1792]{1,0:T(8,128)}) custom-call(bf16[1,64,7168]{2,1,0:T(8,128)(2,1)} %g_hbm.1, f32[1,64,7168]{2,1,0:T(8,128)} %e_hbm.1, f32[32,1792]{1,0:T(8,128)} %bitcast.2), custom_call_target="tpu_custom_call" | custom-call | flops 264241152 | bytes 4587520 | tf_op jit(solution)/shard_map/pallas_call | solution.py:462
  43.0 2.4 %shard_map.51 = (f32[1,64,7168]{2,1,0:T(8,128)}, f32[32,1792]{1,0:T(8,128)}) custom-call(f32[1,64,7168]{2,1,0:T(8,128)} %get-tuple-element.6.out_from, f32[32,1792]{1,0:T(8,128)} %get-tuple-element.7.q_from), custom_call_target="tpu_custom_call" | custom-call | tf_op jit(solution)/shard_map/pallas_call | solution.py:475

commit v7 on v5

--- a/solution.py
+++ b/solution.py
@@ -14,7 +14,7 @@
 BF16 = jnp.bfloat16
 NT = (((1,), (1,)), ((), ()))
 NN = (((1,), (0,)), ((), ()))
-N_CHUNKS = 2
+N_CHUNKS = 3
 PLACE_PARTS = 4
 
 
@@ -64,8 +64,24 @@
     oc = 1 - c
     sib = d + 1 - 2 * c
 
-    load_g = pltpu.make_async_copy(g_hbm.at[0], g_v, in_sem.at[0])
-    load_e = pltpu.make_async_copy(e_hbm.at[0], e_v, in_sem.at[1])
+    def at_dp(i):
+        return lax.rem(d + i, n_dp)
+
+    def at_sh(i, core=c):
+        first, second = i % side, i // side
+        across = first + core * (second - first)
+        down = second + core * (first - second)
+        return lax.rem(s // side + down, side) * side + lax.rem(s % side + across, side)
+
+    def at_z(i):
+        return lax.rem(z + i, nz)
+
+    barrier = pltpu.get_barrier_semaphore()
+    for i in range(1, n_dp):
+        pl.semaphore_signal(barrier, inc=1, device_id=(at_dp(i), s), device_id_type=MESH)
+    for i in range(1, n_sh):
+        pl.semaphore_signal(barrier, inc=1, device_id=(d, at_sh(i)), device_id_type=MESH)
+
     q_loads = []
     if aligned:
         for h in range(2):
@@ -78,26 +94,27 @@
         whole_copy = pltpu.make_async_copy(q_hbm, q_v, in_sem.at[2])
         whole_copy.start()
         q_loads.append(whole_copy)
-    load_g.start()
-    load_e.start()
-
-    def at_dp(i):
-        return lax.rem(d + i, n_dp)
-
-    def at_sh(i, core=c):
-        first, second = i % side, i // side
-        across = first + core * (second - first)
-        down = second + core * (first - second)
-        return lax.rem(s // side + down, side) * side + lax.rem(s % side + across, side)
-
-    def at_z(i):
-        return lax.rem(z + i, nz)
-
-    barrier = pltpu.get_barrier_semaphore()
-    for i in range(1, n_dp):
-        pl.semaphore_signal(barrier, inc=1, device_id=(at_dp(i), s), device_id_type=MESH)
-    for i in range(1, n_sh):
-        pl.semaphore_signal(barrier, inc=1, device_id=(d, at_sh(i)), device_id_type=MESH)
+
+    def merged_loads(k, slot):
+        if not aligned:
+            return []
+        columns = pl.ds(pl.multiple_of(k * width, 128), width)
+        return [
+            pltpu.make_async_copy(src.at[0, :, columns], dst.at[k], in_sem.at[4 + 2 * slot + n])
+            for n, (src, dst) in enumerate(((g_hbm, g_v), (e_hbm, e_v)))
+        ]
+
+    order = [(i, oc) for i in range(n_sh)] + [(i, c) for i in range(n_sh)]
+    loads = [merged_loads(2 * at_sh(i, core) + core, slot) for slot, (i, core) in enumerate(order)]
+    if not aligned:
+        loads[0] = [
+            pltpu.make_async_copy(g_hbm.at[0], g_v, in_sem.at[4]),
+            pltpu.make_async_copy(e_hbm.at[0], e_v, in_sem.at[5]),
+        ]
+    for pair in loads:
+        for copy in pair:
+            copy.start()
+
     for q_load in q_loads:
         q_load.wait()
     if not aligned:
@@ -127,21 +144,33 @@
         for i in range(1, n_sh):
             send(part, part, q_s.at[ch, i], q_r.at[ch, s], (d, at_sh(i)))
 
-    load_g.wait()
-    load_e.wait()
-    for k in range(pieces):
-        cols = slice(k * width, (k + 1) * width)
-        mf[k] = g_v[:, cols].astype(F32) + e_v[:, cols]
+    n_rows = mf.shape[1]
+    if not aligned:
+        for copy in loads[0]:
+            copy.wait()
+        for k in range(pieces):
+            cols = slice(k * width, (k + 1) * width)
+            mf[k] = g_v[:, cols].astype(F32) + e_v[:, cols]
+
+    def merge(slot):
+        i, core = order[slot]
+        k = 2 * at_sh(i, core) + core
+        if aligned:
+            for copy in loads[slot]:
+                copy.wait()
+            mf[k] = g_v[k].astype(F32) + e_v[k]
+        return k
 
     swaps = []
     for i in range(n_sh):
-        o = at_sh(i)
-        swap = remote(mf.at[2 * o + oc], mx.at[o], m_s.at[i], m_r.at[o], (sib, s))
+        o = at_sh(i, oc)
+        swap = remote(mf.at[merge(i)], mx.at[o], m_s.at[i], m_r.at[o], (sib, s))
         swap.start()
         swaps.append(swap)
-    n_rows = mf.shape[1]
     for i in range(n_sh):
-        o = at_sh(i)
+        merge(n_sh + i)
+
+    def chip_sum(o, i):
         arrived(mx.at[o], m_s.at[i], m_r.at[o])
         hi, lo = halves(mf[2 * o + c] + mx[o])
         m2[o, :n_rows] = hi
@@ -151,10 +180,13 @@
         hi, lo = halves(q_all[2 * o + c, :, span])
         return dot(jnp.concatenate([hi, lo], axis=0), m2[o, :, span], NT)
 
+    chip_sum(s, 0)
     acc = left_term(s, pl.ds(0, width))
     for ch, span in enumerate(spans):
         for i in range(1, n_sh):
             o = at_sh(i)
+            if ch == 0:
+                chip_sum(o, i)
             arrived(q_all.at[2 * o + c, :, span], q_s.at[ch, i], q_r.at[ch, o])
             acc = acc + left_term(o, span)
     acc = acc[:rank] + acc[rank:]
@@ -185,12 +217,12 @@
         for i in range(1, n_sh):
             o = at_sh(i)
             w_c[o, :, span] = w_term(o, span)
-            send(w_c.at[o, :, span], w_r.at[s, :, span], w_s.at[ch, i], w_rs.at[ch, s], (d, at_sh(i)))
-        if ch == 0:
-            padded = jnp.concatenate([pt, jnp.zeros((128 - rank, n_rows), F32)], axis=0)
-            gbuf[s] = dot(pt, padded, NT, HIGH)
-            for i in range(1, n_sh):
-                send(gbuf.at[s], gbuf.at[s], g_s.at[i], g_r.at[s], (d, at_sh(i)))
+            send(w_c.at[o, :, span], w_r.at[s, :, span], w_s.at[ch, i], w_rs.at[ch, s], (d, o))
+            if ch == 0 and i == 1:
+                padded = jnp.concatenate([pt, jnp.zeros((128 - rank, n_rows), F32)], axis=0)
+                gbuf[s] = dot(pt, padded, NT, HIGH)
+                for j in range(1, n_sh):
+                    send(gbuf.at[s], gbuf.at[s], g_s.at[j], g_r.at[s], (d, at_sh(j)))
     for span in spans:
         w_r[s, :, span] = w_term(s, span)
     for swap in swaps:
@@ -358,8 +390,8 @@
     dma = pltpu.SemaphoreType.DMA
     small = (8, 128)
     scratch = [
-        vm((n_rows, full), BF16),
-        vm((n_rows, full), F32),
+        vm((pieces, n_rows, width) if aligned else (n_rows, full), BF16),
+        vm((pieces, n_rows, width) if aligned else (n_rows, full), F32),
         vm(small if aligned else (rank, share), F32),
         vm((n_sh, 2 * n_rows, width), BF16),
         vm((pieces, n_rows, width), F32),
@@ -375,7 +407,7 @@
         vm((pieces, rank, width), F32),
         vm(small if aligned else (n_rows, full), F32),
         vm(small if aligned else (rank, share), F32),
-        dma((4,)),
+        dma((4 + 2 * pieces,)),
     ]
     n_ch = len(chunks)
     per_chunk = [(n_ch, n_sh), (n_dp,), (n_sh,), (n_sh,), (n_ch, n_sh)] + [(n_ch, nz)] * 2 + [(n_ch, n_sh)] * 2

time: 44.7 us -> 46.2 us (1.034)
  Pallas kernels: 43.9 us -> 45.1 us
    pallas_call x1, Pallas kernels: 41.4 us -> 42.6 us  [per_device(): pl.pallas_call(functools.partial(kernel, dims, chunks), out_shape=shapes,...]
where the time goes in v7:
time: 46.2 us; the launch traced here: 45.7 us
  Pallas kernels  45.1 us (98%)
  between operations  0.64 us (1%)
    pallas_call x1, Pallas kernels, per_device(): pl.pallas_call(functools.partial(kernel, dims, chunks), out_shape=shapes,...  42.6 us
    pallas_call x1, Pallas kernels, per_device(): pl.pallas_call(place, out_shape=shapes, in_specs=[hbm, hbm], out_specs=(h...  2.45 us

profile of v7, /device:TPU:0, one launch (start us, length us, event | category | flops | bytes accessed | tf_op | source)
XLA Modules:
  0.0 45.7 jit_solution(11672048630319395977)
XLA Ops:
  0.6 42.6 %shard_map.50 = (f32[1,64,7168]{2,1,0:T(8,128)}, f32[32,1792]{1,0:T(8,128)}) custom-call(bf16[1,64,7168]{2,1,0:T(8,128)(2,1)} %g_hbm.1, f32[1,64,7168]{2,1,0:T(8,128)} %e_hbm.1, f32[32,1792]{1,0:T(8,128)} %bitcast.2), custom_call_target="tpu_custom_call" | custom-call | flops 264241152 | bytes 4587520 | tf_op jit(solution)/shard_map/pallas_call | solution.py:422
  43.3 2.4 %shard_map.51 = (f32[1,64,7168]{2,1,0:T(8,128)}, f32[32,1792]{1,0:T(8,128)}) custom-call(f32[1,64,7168]{2,1,0:T(8,128)} %get-tuple-element.6.out_from, f32[32,1792]{1,0:T(8,128)} %get-tuple-element.7.q_from), custom_call_target="tpu_custom_call" | custom-call | tf_op jit(solution)/shard_map/pallas_call | solution.py:435

commit v8 on v5

--- a/solution.py
+++ b/solution.py
@@ -59,10 +59,41 @@
     pieces = 2 * n_sh
     d = lax.axis_index("dp")
     s = lax.axis_index("shard")
-    z = d // 2
-    c = d % 2
+    z = lax.div(d, 2)
+    c = lax.rem(d, 2)
     oc = 1 - c
     sib = d + 1 - 2 * c
+
+    def ring(at, count):
+        places = [at]
+        for _ in range(count - 1):
+            step = places[-1] + 1
+            places.append(jnp.where(step == count, 0, step))
+        return places
+
+    dp_at = ring(d, n_dp)
+    z_at = ring(z, nz)
+    rows_at = ring(lax.div(s, side), side)
+    cols_at = ring(lax.rem(s, side), side)
+    in_rows = [rows_at[i // side] * side + cols_at[i % side] for i in range(n_sh)]
+    in_cols = [rows_at[i % side] * side + cols_at[i // side] for i in range(n_sh)]
+    mine_at = [jnp.where(c == 0, a, b) for a, b in zip(in_rows, in_cols)]
+    theirs_at = [jnp.where(c == 0, b, a) for a, b in zip(in_rows, in_cols)]
+
+    def at_dp(i):
+        return dp_at[i]
+
+    def at_sh(i, core=None):
+        return mine_at[i] if core is None else theirs_at[i]
+
+    def at_z(i):
+        return z_at[i]
+
+    barrier = pltpu.get_barrier_semaphore()
+    for i in range(1, n_dp):
+        pl.semaphore_signal(barrier, inc=1, device_id=(at_dp(i), s), device_id_type=MESH)
+    for i in range(1, n_sh):
+        pl.semaphore_signal(barrier, inc=1, device_id=(d, at_sh(i)), device_id_type=MESH)
 
     load_g = pltpu.make_async_copy(g_hbm.at[0], g_v, in_sem.at[0])
     load_e = pltpu.make_async_copy(e_hbm.at[0], e_v, in_sem.at[1])
@@ -81,23 +112,6 @@
     load_g.start()
     load_e.start()
 
-    def at_dp(i):
-        return lax.rem(d + i, n_dp)
-
-    def at_sh(i, core=c):
-        first, second = i % side, i // side
-        across = first + core * (second - first)
-        down = second + core * (first - second)
-        return lax.rem(s // side + down, side) * side + lax.rem(s % side + across, side)
-
-    def at_z(i):
-        return lax.rem(z + i, nz)
-
-    barrier = pltpu.get_barrier_semaphore()
-    for i in range(1, n_dp):
-        pl.semaphore_signal(barrier, inc=1, device_id=(at_dp(i), s), device_id_type=MESH)
-    for i in range(1, n_sh):
-        pl.semaphore_signal(barrier, inc=1, device_id=(d, at_sh(i)), device_id_type=MESH)
     for q_load in q_loads:
         q_load.wait()
     if not aligned:
@@ -122,10 +136,8 @@
 
     mine = 2 * s + c
     other = 2 * s + oc
-    for ch, span in enumerate(spans):
-        part = q_all.at[mine, :, span]
-        for i in range(1, n_sh):
-            send(part, part, q_s.at[ch, i], q_r.at[ch, s], (d, at_sh(i)))
+    for i in range(1, n_sh):
+        send(q_all.at[mine], q_all.at[mine], q_s.at[i], q_r.at[s], (d, at_sh(i)))
 
     load_g.wait()
     load_e.wait()
@@ -135,28 +147,23 @@
 
     swaps = []
     for i in range(n_sh):
-        o = at_sh(i)
+        o = at_sh(i, oc)
         swap = remote(mf.at[2 * o + oc], mx.at[o], m_s.at[i], m_r.at[o], (sib, s))
         swap.start()
         swaps.append(swap)
     n_rows = mf.shape[1]
+    acc = None
     for i in range(n_sh):
         o = at_sh(i)
         arrived(mx.at[o], m_s.at[i], m_r.at[o])
         hi, lo = halves(mf[2 * o + c] + mx[o])
         m2[o, :n_rows] = hi
         m2[o, n_rows:] = lo
-
-    def left_term(o, span):
-        hi, lo = halves(q_all[2 * o + c, :, span])
-        return dot(jnp.concatenate([hi, lo], axis=0), m2[o, :, span], NT)
-
-    acc = left_term(s, pl.ds(0, width))
-    for ch, span in enumerate(spans):
-        for i in range(1, n_sh):
-            o = at_sh(i)
-            arrived(q_all.at[2 * o + c, :, span], q_s.at[ch, i], q_r.at[ch, o])
-            acc = acc + left_term(o, span)
+        if i > 0:
+            arrived(q_all.at[2 * o + c], q_s.at[i], q_r.at[o])
+        hi, lo = halves(q_all[2 * o + c])
+        term = dot(jnp.concatenate([hi, lo], axis=0), m2[o], NT)
+        acc = term if acc is None else acc + term
     acc = acc[:rank] + acc[rank:]
     part = acc[:, :n_rows] + acc[:, n_rows:]
     half = rank // 2
@@ -185,12 +192,12 @@
         for i in range(1, n_sh):
             o = at_sh(i)
             w_c[o, :, span] = w_term(o, span)
-            send(w_c.at[o, :, span], w_r.at[s, :, span], w_s.at[ch, i], w_rs.at[ch, s], (d, at_sh(i)))
-        if ch == 0:
-            padded = jnp.concatenate([pt, jnp.zeros((128 - rank, n_rows), F32)], axis=0)
-            gbuf[s] = dot(pt, padded, NT, HIGH)
-            for i in range(1, n_sh):
-                send(gbuf.at[s], gbuf.at[s], g_s.at[i], g_r.at[s], (d, at_sh(i)))
+            send(w_c.at[o, :, span], w_r.at[s, :, span], w_s.at[ch, i], w_rs.at[ch, s], (d, o))
+            if ch == 0 and i == 1:
+                padded = jnp.concatenate([pt, jnp.zeros((128 - rank, n_rows), F32)], axis=0)
+                gbuf[s] = dot(pt, padded, NT, HIGH)
+                for j in range(1, n_sh):
+                    send(gbuf.at[s], gbuf.at[s], g_s.at[j], g_r.at[s], (d, at_sh(j)))
     for span in spans:
         w_r[s, :, span] = w_term(s, span)
     for swap in swaps:
@@ -378,7 +385,7 @@
         dma((4,)),
     ]
     n_ch = len(chunks)
-    per_chunk = [(n_ch, n_sh), (n_dp,), (n_sh,), (n_sh,), (n_ch, n_sh)] + [(n_ch, nz)] * 2 + [(n_ch, n_sh)] * 2
+    per_chunk = [(n_sh,), (n_dp,), (n_sh,), (n_sh,), (n_ch, n_sh)] + [(n_ch, nz)] * 2 + [(n_ch, n_sh)] * 2
     for shape in per_chunk:
         scratch += [dma(shape), dma(shape)]
     scratch += [dma((n_ch * pieces,)), dma((2,))]

time: 44.7 us -> 43.6 us (0.975)
  Pallas kernels: 43.9 us -> 42.8 us
    pallas_call x1, Pallas kernels: 41.4 us -> 40.4 us  [per_device(): pl.pallas_call(functools.partial(kernel, dims, chunks), out_shape=shapes,...]
where the time goes in v8:
time: 43.6 us; the launch traced here: 43.4 us
  Pallas kernels  42.8 us (98%)
  between operations  0.64 us (1%)
    pallas_call x1, Pallas kernels, per_device(): pl.pallas_call(functools.partial(kernel, dims, chunks), out_shape=shapes,...  40.4 us
    pallas_call x1, Pallas kernels, per_device(): pl.pallas_call(place, out_shape=shapes, in_specs=[hbm, hbm], out_specs=(h...  2.45 us

profile of v8, /device:TPU:0, one launch (start us, length us, event | category | flops | bytes accessed | tf_op | source)
XLA Modules:
  0.0 43.4 jit_solution(6811817416799555647)
XLA Ops:
  0.6 40.4 %shard_map.50 = (f32[1,64,7168]{2,1,0:T(8,128)}, f32[32,1792]{1,0:T(8,128)}) custom-call(bf16[1,64,7168]{2,1,0:T(8,128)(2,1)} %g_hbm.1, f32[1,64,7168]{2,1,0:T(8,128)} %e_hbm.1, f32[32,1792]{1,0:T(8,128)} %bitcast.2), custom_call_target="tpu_custom_call" | custom-call | flops 264241152 | bytes 4587520 | tf_op jit(solution)/shard_map/pallas_call | solution.py:397
  41.0 2.4 %shard_map.51 = (f32[1,64,7168]{2,1,0:T(8,128)}, f32[32,1792]{1,0:T(8,128)}) custom-call(f32[1,64,7168]{2,1,0:T(8,128)} %get-tuple-element.6.out_from, f32[32,1792]{1,0:T(8,128)} %get-tuple-element.7.q_from), custom_call_target="tpu_custom_call" | custom-call | tf_op jit(solution)/shard_map/pallas_call | solution.py:410

commit v9 on v8

--- a/solution.py
+++ b/solution.py
@@ -125,6 +125,11 @@
         )
 
     sends = []
+    stores = []
+
+    def lanes(start, ch):
+        first, last = chunks[ch]
+        return pl.ds(pl.multiple_of(start + first, 128), last - first)
 
     def send(src, dst, send_sem, recv_sem, target):
         copy = remote(src, dst, send_sem, recv_sem, target)
@@ -266,7 +271,14 @@
         part = y_all.at[mine, :, span]
         for i in range(1, n_sh):
             send(part, part, y_s.at[ch, i], y_r.at[ch, s], (d, at_sh(i)))
-        send(part, part, yc_s.at[ch, 0], yc_r.at[ch, s], (sib, s))
+        if aligned:
+            target = qnew_hbm.at[:, lanes(c * width, ch)]
+            send(part, target, yc_s.at[ch, n_sh], yc_r.at[ch, n_sh], (sib, s))
+            copy = pltpu.make_async_copy(part, target, qn_sem.at[ch])
+            copy.start()
+            stores.append(copy)
+        else:
+            send(part, part, yc_s.at[ch, n_sh], yc_r.at[ch, n_sh], (sib, s))
 
     for step in range(n_ch + 2):
         if step < n_ch:
@@ -276,49 +288,44 @@
         if 0 <= step - 2 < n_ch:
             share_out(step - 2, spans[step - 2])
 
-    stores = []
-
-    def finish(k, ch):
-        lo_lane, hi_lane = chunks[ch]
-        hi, lo = halves(y_all[k, :, spans[ch]])
-        mf[k, :, spans[ch]] = mf[k, :, spans[ch]] - dot(ph3, jnp.concatenate([hi, lo, hi], axis=0))
+    def finish(i, ch):
+        o = at_sh(i)
+        k = 2 * o + c
+        span = spans[ch]
+        hi, lo = halves(y_all[k, :, span])
+        product = dot(ph3, jnp.concatenate([hi, lo, hi], axis=0))
+        mx[o, :, span] = mx[o, :, span] - product
+        theirs = out_hbm.at[0, :, lanes(k * width, ch)] if aligned else mf.at[k, :, span]
+        send(mx.at[o, :, span], theirs, yc_s.at[ch, i], yc_r.at[ch, o], (sib, s))
+        mf[k, :, span] = mf[k, :, span] - product
         if aligned:
-            columns = pl.ds(pl.multiple_of(k * width + lo_lane, 128), hi_lane - lo_lane)
-            copy = pltpu.make_async_copy(
-                mf.at[k, :, spans[ch]], out_hbm.at[0, :, columns], out_sem.at[len(stores)]
-            )
+            copy = pltpu.make_async_copy(mf.at[k, :, span], theirs, out_sem.at[ch, i])
             copy.start()
             stores.append(copy)
 
-    for ch, span in enumerate(spans):
-        finish(mine, ch)
-        arrived(y_all.at[other, :, span], yc_s.at[ch, 0], yc_r.at[ch, s])
-        finish(other, ch)
-    late = []
-    for h in range(2):
-        if aligned:
-            target = qnew_hbm.at[:, h * width : (h + 1) * width]
-            copy = pltpu.make_async_copy(y_all.at[2 * s + h], target, qn_sem.at[h])
-            copy.start()
-            late.append(copy)
-        else:
-            qn_v[:, h * width : (h + 1) * width] = y_all[2 * s + h]
+    for ch in range(n_ch):
+        finish(0, ch)
     for ch, span in enumerate(spans):
         for i in range(1, n_sh):
             o = at_sh(i)
-            part = y_all.at[2 * o + c, :, span]
-            arrived(part, y_s.at[ch, i], y_r.at[ch, o])
-            send(part, part, yc_s.at[ch, i], yc_r.at[ch, o], (sib, s))
-        for i in range(1, n_sh):
-            finish(2 * at_sh(i) + c, ch)
-        for i in range(1, n_sh):
+            arrived(y_all.at[2 * o + c, :, span], y_s.at[ch, i], y_r.at[ch, o])
+            finish(i, ch)
+    for ch, span in enumerate(spans):
+        q_part = qnew_hbm.at[:, lanes(oc * width, ch)] if aligned else y_all.at[other, :, span]
+        arrived(q_part, yc_s.at[ch, n_sh], yc_r.at[ch, n_sh])
+        for i in range(n_sh):
             o = at_sh(i, oc)
-            arrived(y_all.at[2 * o + oc, :, span], yc_s.at[ch, i], yc_r.at[ch, o])
-            finish(2 * o + oc, ch)
+            k = 2 * o + oc
+            part = out_hbm.at[0, :, lanes(k * width, ch)] if aligned else mf.at[k, :, span]
+            arrived(part, yc_s.at[ch, i], yc_r.at[ch, o])
+    late = []
+    if not aligned:
+        for h in range(2):
+            qn_v[:, h * width : (h + 1) * width] = y_all[2 * s + h]
     if not aligned:
         for k in range(pieces):
             out_v[:, k * width : (k + 1) * width] = mf[k]
-        for src, dst, sem in ((out_v, out_hbm.at[0], out_sem.at[0]), (qn_v, qnew_hbm, qn_sem.at[0])):
+        for src, dst, sem in ((out_v, out_hbm.at[0], out_sem.at[0, 0]), (qn_v, qnew_hbm, qn_sem.at[0])):
             copy = pltpu.make_async_copy(src, dst, sem)
             copy.start()
             late.append(copy)
@@ -386,9 +393,10 @@
     ]
     n_ch = len(chunks)
     per_chunk = [(n_sh,), (n_dp,), (n_sh,), (n_sh,), (n_ch, n_sh)] + [(n_ch, nz)] * 2 + [(n_ch, n_sh)] * 2
+    per_chunk[-1] = (n_ch, n_sh + 1)
     for shape in per_chunk:
         scratch += [dma(shape), dma(shape)]
-    scratch += [dma((n_ch * pieces,)), dma((2,))]
+    scratch += [dma((n_ch, n_sh)), dma((max(n_ch, 2),))]
     shapes = (
         jax.ShapeDtypeStruct((1, n_rows, full), F32),
         jax.ShapeDtypeStruct((rank, share), F32),

time: 43.6 us -> 42.5 us (0.975)
  Pallas kernels: 42.8 us -> 41.7 us
    pallas_call x1, Pallas kernels: 40.4 us -> 39.3 us  [per_device(): pl.pallas_call(functools.partial(kernel, dims, chunks), out_shape=shapes,...]
where the time goes in v9:
time: 42.5 us; the launch traced here: 42.4 us
  Pallas kernels  41.7 us (98%)
  between operations  0.64 us (2%)
    pallas_call x1, Pallas kernels, per_device(): pl.pallas_call(functools.partial(kernel, dims, chunks), out_shape=shapes,...  39.3 us
    pallas_call x1, Pallas kernels, per_device(): pl.pallas_call(place, out_shape=shapes, in_specs=[hbm, hbm], out_specs=(h...  2.45 us

profile of v9, /device:TPU:0, one launch (start us, length us, event | category | flops | bytes accessed | tf_op | source)
XLA Modules:
  0.0 42.4 jit_solution(1611930109400718463)
XLA Ops:
  0.6 39.3 %shard_map.50 = (f32[1,64,7168]{2,1,0:T(8,128)}, f32[32,1792]{1,0:T(8,128)}) custom-call(bf16[1,64,7168]{2,1,0:T(8,128)(2,1)} %g_hbm.1, f32[1,64,7168]{2,1,0:T(8,128)} %e_hbm.1, f32[32,1792]{1,0:T(8,128)} %bitcast.2), custom_call_target="tpu_custom_call" | custom-call | flops 264241152 | bytes 4587520 | tf_op jit(solution)/shard_map/pallas_call | solution.py:405
  39.9 2.4 %shard_map.51 = (f32[1,64,7168]{2,1,0:T(8,128)}, f32[32,1792]{1,0:T(8,128)}) custom-call(f32[1,64,7168]{2,1,0:T(8,128)} %get-tuple-element.6.out_from, f32[32,1792]{1,0:T(8,128)} %get-tuple-element.7.q_from), custom_call_target="tpu_custom_call" | custom-call | tf_op jit(solution)/shard_map/pallas_call | solution.py:418

commit v10 on v9

--- a/solution.py
+++ b/solution.py
@@ -146,17 +146,27 @@
 
     load_g.wait()
     load_e.wait()
-    for k in range(pieces):
-        cols = slice(k * width, (k + 1) * width)
+    n_rows = mf.shape[1]
+
+    def merge(k):
+        cols = pl.ds(pl.multiple_of(k * width, 128), width) if aligned else pl.ds(k * width, width)
         mf[k] = g_v[:, cols].astype(F32) + e_v[:, cols]
+
+    if not aligned:
+        for k in range(pieces):
+            merge(k)
 
     swaps = []
     for i in range(n_sh):
         o = at_sh(i, oc)
+        if aligned:
+            merge(2 * o + oc)
         swap = remote(mf.at[2 * o + oc], mx.at[o], m_s.at[i], m_r.at[o], (sib, s))
         swap.start()
         swaps.append(swap)
-    n_rows = mf.shape[1]
+    if aligned:
+        for i in range(n_sh):
+            merge(2 * at_sh(i) + c)
     acc = None
     for i in range(n_sh):
         o = at_sh(i)
@@ -207,24 +217,6 @@
         w_r[s, :, span] = w_term(s, span)
     for swap in swaps:
         swap.wait_send()
-
-    for i in range(1, n_sh):
-        o = at_sh(i)
-        arrived(gbuf.at[o], g_s.at[i], g_r.at[o])
-    gram = gbuf[0]
-    for k in range(1, n_sh):
-        gram = gram + gbuf[k]
-    linv = inverse_factor(gram)
-    p_hat_t = dot(linv, pt, NN, HIGH)
-    three = jnp.concatenate([p_hat_t, p_hat_t, p_hat_t], axis=0)
-    rounded = three.astype(BF16).astype(F32)
-    row = lax.broadcasted_iota(jnp.int32, three.shape, 0)
-    ph3 = jnp.where(row < 2 * rank, rounded, three - rounded).T.astype(BF16)
-
-    l3 = jnp.concatenate([linv, linv, linv], axis=1)
-    l_rounded = l3.astype(BF16).astype(F32)
-    lane = lax.broadcasted_iota(jnp.int32, l3.shape, 1)
-    l3 = jnp.where(lane < 2 * rank, l_rounded, l3 - l_rounded).astype(BF16)
 
     def over_shards(ch, span):
         for i in range(1, n_sh):
@@ -258,6 +250,20 @@
                 send(part, part, za_s.at[ch, i], za_r.at[ch, z], (2 * at_z(i) + c, s))
         else:
             z_full[0, :, span] = r
+
+    over_shards(0, spans[0])
+
+    for i in range(1, n_sh):
+        o = at_sh(i)
+        arrived(gbuf.at[o], g_s.at[i], g_r.at[o])
+    gram = gbuf[0]
+    for k in range(1, n_sh):
+        gram = gram + gbuf[k]
+    linv = inverse_factor(gram)
+    l3 = jnp.concatenate([linv, linv, linv], axis=1)
+    l_rounded = l3.astype(BF16).astype(F32)
+    lane = lax.broadcasted_iota(jnp.int32, l3.shape, 1)
+    l3 = jnp.where(lane < 2 * rank, l_rounded, l3 - l_rounded).astype(BF16)
 
     def share_out(ch, span):
         r = z_full[0, :, span]
@@ -281,12 +287,18 @@
             send(part, part, yc_s.at[ch, n_sh], yc_r.at[ch, n_sh], (sib, s))
 
     for step in range(n_ch + 2):
-        if step < n_ch:
+        if 0 < step < n_ch:
             over_shards(step, spans[step])
         if 0 <= step - 1 < n_ch:
             over_z(step - 1, spans[step - 1])
         if 0 <= step - 2 < n_ch:
             share_out(step - 2, spans[step - 2])
+
+    p_hat_t = dot(linv, pt, NN, HIGH)
+    three = jnp.concatenate([p_hat_t, p_hat_t, p_hat_t], axis=0)
+    rounded = three.astype(BF16).astype(F32)
+    row = lax.broadcasted_iota(jnp.int32, three.shape, 0)
+    ph3 = jnp.where(row < 2 * rank, rounded, three - rounded).T.astype(BF16)
 
     def finish(i, ch):
         o = at_sh(i)

time: 42.5 us -> 42.5 us (level)
  no operation moved by 1% of the time
where the time goes in v10:
time: 42.5 us; the launch traced here: 42.4 us
  Pallas kernels  41.7 us (98%)
  between operations  0.64 us (2%)
    pallas_call x1, Pallas kernels, per_device(): pl.pallas_call(functools.partial(kernel, dims, chunks), out_shape=shapes,...  39.3 us
    pallas_call x1, Pallas kernels, per_device(): pl.pallas_call(place, out_shape=shapes, in_specs=[hbm, hbm], out_specs=(h...  2.45 us

profile of v10, /device:TPU:0, one launch (start us, length us, event | category | flops | bytes accessed | tf_op | source)
XLA Modules:
  0.0 42.4 jit_solution(1958056527837174447)
XLA Ops:
  0.6 39.3 %shard_map.50 = (f32[1,64,7168]{2,1,0:T(8,128)}, f32[32,1792]{1,0:T(8,128)}) custom-call(bf16[1,64,7168]{2,1,0:T(8,128)(2,1)} %g_hbm.1, f32[1,64,7168]{2,1,0:T(8,128)} %e_hbm.1, f32[32,1792]{1,0:T(8,128)} %bitcast.2), custom_call_target="tpu_custom_call" | custom-call | flops 264241152 | bytes 4587520 | tf_op jit(solution)/shard_map/pallas_call | solution.py:417
  39.9 2.4 %shard_map.51 = (f32[1,64,7168]{2,1,0:T(8,128)}, f32[32,1792]{1,0:T(8,128)}) custom-call(f32[1,64,7168]{2,1,0:T(8,128)} %get-tuple-element.6.out_from, f32[32,1792]{1,0:T(8,128)} %get-tuple-element.7.q_from), custom_call_target="tpu_custom_call" | custom-call | tf_op jit(solution)/shard_map/pallas_call | solution.py:430

commit v11 on v10

--- a/solution.py
+++ b/solution.py
@@ -15,7 +15,7 @@
 NT = (((1,), (1,)), ((), ()))
 NN = (((1,), (0,)), ((), ()))
 N_CHUNKS = 2
-PLACE_PARTS = 4
+PLACE_PARTS = 8
 
 
 def dot(a, b, dims=NN, precision=None):
@@ -125,16 +125,17 @@
         )
 
     sends = []
+    last_sends = []
     stores = []
 
     def lanes(start, ch):
         first, last = chunks[ch]
         return pl.ds(pl.multiple_of(start + first, 128), last - first)
 
-    def send(src, dst, send_sem, recv_sem, target):
+    def send(src, dst, send_sem, recv_sem, target, kept=sends):
         copy = remote(src, dst, send_sem, recv_sem, target)
         copy.start()
-        sends.append(copy)
+        kept.append(copy)
 
     def arrived(dst, send_sem, recv_sem):
         remote(dst, dst, send_sem, recv_sem, (sib, s)).wait_recv()
@@ -276,15 +277,15 @@
         y_all[mine, :, span] = dot(l3, jnp.concatenate([hi, lo, hi], axis=0))
         part = y_all.at[mine, :, span]
         for i in range(1, n_sh):
-            send(part, part, y_s.at[ch, i], y_r.at[ch, s], (d, at_sh(i)))
+            send(part, part, y_s.at[ch, i], y_r.at[ch, s], (d, at_sh(i)), last_sends)
         if aligned:
             target = qnew_hbm.at[:, lanes(c * width, ch)]
-            send(part, target, yc_s.at[ch, n_sh], yc_r.at[ch, n_sh], (sib, s))
+            send(part, target, yc_s.at[ch, n_sh], yc_r.at[ch, n_sh], (sib, s), last_sends)
             copy = pltpu.make_async_copy(part, target, qn_sem.at[ch])
             copy.start()
             stores.append(copy)
         else:
-            send(part, part, yc_s.at[ch, n_sh], yc_r.at[ch, n_sh], (sib, s))
+            send(part, part, yc_s.at[ch, n_sh], yc_r.at[ch, n_sh], (sib, s), last_sends)
 
     for step in range(n_ch + 2):
         if 0 < step < n_ch:
@@ -308,7 +309,7 @@
         product = dot(ph3, jnp.concatenate([hi, lo, hi], axis=0))
         mx[o, :, span] = mx[o, :, span] - product
         theirs = out_hbm.at[0, :, lanes(k * width, ch)] if aligned else mf.at[k, :, span]
-        send(mx.at[o, :, span], theirs, yc_s.at[ch, i], yc_r.at[ch, o], (sib, s))
+        send(mx.at[o, :, span], theirs, yc_s.at[ch, i], yc_r.at[ch, o], (sib, s), last_sends)
         mf[k, :, span] = mf[k, :, span] - product
         if aligned:
             copy = pltpu.make_async_copy(mf.at[k, :, span], theirs, out_sem.at[ch, i])
@@ -317,6 +318,8 @@
 
     for ch in range(n_ch):
         finish(0, ch)
+    for copy in sends:
+        copy.wait_send()
     for ch, span in enumerate(spans):
         for i in range(1, n_sh):
             o = at_sh(i)
@@ -341,7 +344,7 @@
             copy = pltpu.make_async_copy(src, dst, sem)
             copy.start()
             late.append(copy)
-    for copy in sends:
+    for copy in last_sends:
         copy.wait_send()
     for copy in stores + late:
         copy.wait()

time: 42.5 us -> 42.6 us (level)
  no operation moved by 1% of the time
where the time goes in v11:
time: 42.6 us; the launch traced here: 42.4 us
  Pallas kernels  41.8 us (98%)
  between operations  0.64 us (2%)
    pallas_call x1, Pallas kernels, per_device(): pl.pallas_call(functools.partial(kernel, dims, chunks), out_shape=shapes,...  39.3 us
    pallas_call x1, Pallas kernels, per_device(): pl.pallas_call(place, out_shape=shapes, in_specs=[hbm, hbm], out_specs=(h...  2.5 us

profile of v11, /device:TPU:0, one launch (start us, length us, event | category | flops | bytes accessed | tf_op | source)
XLA Modules:
  0.0 42.4 jit_solution(5221385346218308889)
XLA Ops:
  0.6 39.3 %shard_map.50 = (f32[1,64,7168]{2,1,0:T(8,128)}, f32[32,1792]{1,0:T(8,128)}) custom-call(bf16[1,64,7168]{2,1,0:T(8,128)(2,1)} %g_hbm.1, f32[1,64,7168]{2,1,0:T(8,128)} %e_hbm.1, f32[32,1792]{1,0:T(8,128)} %bitcast.2), custom_call_target="tpu_custom_call" | custom-call | flops 264241152 | bytes 4587520 | tf_op jit(solution)/shard_map/pallas_call | solution.py:420
  39.9 2.5 %shard_map.51 = (f32[1,64,7168]{2,1,0:T(8,128)}, f32[32,1792]{1,0:T(8,128)}) custom-call(f32[1,64,7168]{2,1,0:T(8,128)} %get-tuple-element.6.out_from, f32[32,1792]{1,0:T(8,128)} %get-tuple-element.7.q_from), custom_call_target="tpu_custom_call" | custom-call | tf_op jit(solution)/shard_map/pallas_call | solution.py:433

commit v12 on v11

--- a/solution.py
+++ b/solution.py
@@ -14,7 +14,7 @@
 BF16 = jnp.bfloat16
 NT = (((1,), (1,)), ((), ()))
 NN = (((1,), (0,)), ((), ()))
-N_CHUNKS = 2
+N_CHUNKS = 1
 PLACE_PARTS = 8
 
 

time: 42.6 us -> 44.7 us (1.049)
  Pallas kernels: 41.8 us -> 43.9 us
    pallas_call x1, Pallas kernels: 39.3 us -> 41.4 us  [per_device(): pl.pallas_call(functools.partial(kernel, dims, chunks), out_shape=shapes,...]
where the time goes in v12:
time: 44.7 us; the launch traced here: 44.6 us
  Pallas kernels  43.9 us (98%)
  between operations  0.64 us (1%)
    pallas_call x1, Pallas kernels, per_device(): pl.pallas_call(functools.partial(kernel, dims, chunks), out_shape=shapes,...  41.4 us
    pallas_call x1, Pallas kernels, per_device(): pl.pallas_call(place, out_shape=shapes, in_specs=[hbm, hbm], out_specs=(h...  2.5 us

profile of v12, /device:TPU:0, one launch (start us, length us, event | category | flops | bytes accessed | tf_op | source)
XLA Modules:
  0.0 44.6 jit_solution(17066926964130980392)
XLA Ops:
  0.6 41.4 %shard_map.50 = (f32[1,64,7168]{2,1,0:T(8,128)}, f32[32,1792]{1,0:T(8,128)}) custom-call(bf16[1,64,7168]{2,1,0:T(8,128)(2,1)} %g_hbm.1, f32[1,64,7168]{2,1,0:T(8,128)} %e_hbm.1, f32[32,1792]{1,0:T(8,128)} %bitcast.2), custom_call_target="tpu_custom_call" | custom-call | flops 264241152 | bytes 4587520 | tf_op jit(solution)/shard_map/pallas_call | solution.py:420
  42.1 2.5 %shard_map.51 = (f32[1,64,7168]{2,1,0:T(8,128)}, f32[32,1792]{1,0:T(8,128)}) custom-call(f32[1,64,7168]{2,1,0:T(8,128)} %get-tuple-element.6.out_from, f32[32,1792]{1,0:T(8,128)} %get-tuple-element.7.q_from), custom_call_target="tpu_custom_call" | custom-call | tf_op jit(solution)/shard_map/pallas_call | solution.py:433
